TPU v7x, 128 devices: a whole 4x4x4 slice. The times are simulated.
128 devices in a mesh: space: 32 (over x, y, core), rank: 4 (over z).
Axes of the slice: x: 4, y: 4, z: 4, core: 2. Of those that a mesh axis runs over, the one named last changes fastest.
Arguments:
- xfactor: float32 [128, 524288], P('rank', 'space'), may hold values from -6 to 6
- volume: float32 [3, 64, 64], replicated, may hold values from -0.75 to 0.75
- upwind: float32 [3, 64, 64], replicated, may hold values from -0.75 to 0.75
- neighbor: int32 [3, 8192], P(None, 'space'), may hold values from -1 to 8190, as said below
- coeffs: float32 [512, 128], replicated, may hold values from -0.25 to 0.25
Outputs:
- new_factor: float32 [128, 524288], P(None, ('space', 'rank'))
- r_factor: float32 [512, 512], replicated
Inputs may be any that keep to these rules, and one draw needn't show every extreme that they name: neighbor[d, e] is -1 or an element between e - 32 and e - 1; the distance 32 occurs in every direction.
All inputs are finite; a program needn't handle non-finite values.
Results may differ from a plain program's by a relative error of at most 0.0001.
Values sent between devices are 32-bit elements; how exact they have to be, the bound alone decides.
No kernel may reach another device: no remote copies, remote signals or barrier semaphores. Data moves between devices by JAX's collectives and lax.ppermute only.
A program may use at most 128 MiB of HBM per device.

v0:
```python
import functools

import jax
import jax.numpy as jnp
from jax import lax
from jax.experimental import pallas as pl
from jax.experimental.pallas import tpu as pltpu
from jax.sharding import Mesh
from jax.sharding import PartitionSpec as P

SPACE_RANK = ("x", "y", "core", "rank")
SPACE = ("x", "y", "core")
HALO_EL = 32
F32, BF16 = jnp.float32, jnp.bfloat16
VMEM = pl.BlockSpec(memory_space=pltpu.VMEM)
SMEM = pl.BlockSpec(memory_space=pltpu.SMEM)
ANY = pl.BlockSpec(memory_space=pl.ANY)


def halves(x):
    high = x.astype(BF16)
    return high, (x - high.astype(F32)).astype(BF16)


def product(a, b, over):
    dims = (((over[0],), (over[1],)), ((), ()))
    return lax.dot_general(a, b, dims, preferred_element_type=F32)


def exact(a, b, over):
    dims = (((over[0],), (over[1],)), ((), ()))
    return lax.dot_general(
        a, b, dims, precision=lax.Precision.HIGHEST, preferred_element_type=F32
    )


TILES = 32
ZERO_TILE = 2 * TILES
WIDE = 2048


def transport_kernel(second, place, index, xfactor, *refs):
    mains, refs = refs[:3], refs[3:]
    above, refs = ((), refs) if second else (refs[:4], refs[4:])
    before, refs = (None, refs) if second else (refs[0], refs[1:])
    volume, upwind, gram, cand = refs[:4]
    window, mats_high, mats_low, tiles_high, tiles_low = refs[4:9]
    c_high, c_low, same, cross, in_sems, out_sems = refs[9:]

    copies = []
    own = pl.multiple_of(place[0] * 2 * WIDE, 2 * WIDE)
    for piece in range(4):
        if piece == 0:
            sources = [xfactor.at[:, pl.ds(own, WIDE)], xfactor.at[:, pl.ds(own + WIDE, WIDE)]]
        else:
            sources = [mains[piece - 1].at[:, 0:WIDE], mains[piece - 1].at[:, WIDE : 2 * WIDE]]
        if not second:
            sources = [above[piece], sources[0]]
        for side in range(2):
            to = window.at[piece, :, side * WIDE : side * WIDE + WIDE]
            copies.append(pltpu.make_async_copy(sources[side], to, in_sems.at[2 * piece + side]))
    for copy in copies:
        copy.start()

    lane = lax.broadcasted_iota(jnp.int32, (64, 128), 1)
    mats_high[...] = jnp.zeros_like(mats_high)
    mats_low[...] = jnp.zeros_like(mats_low)
    for direc in range(3):
        for side, block in enumerate((volume, upwind)):
            wide = jnp.concatenate([block[direc], block[direc]], axis=1)
            for spot in range(4):
                keep = (lane < 64) if spot % 2 == 0 else (lane >= 64)
                rows = slice(64 * spot, 64 * spot + 64)
                start = 256 * side + 128 * (spot // 2)
                high, low = halves(jnp.where(keep, wide, 0.0))
                mats_high[direc, rows, start : start + 128] = high
                mats_low[direc, rows, start : start + 128] = low
    tiles_high[ZERO_TILE] = jnp.zeros((128, 128), BF16)
    tiles_low[ZERO_TILE] = jnp.zeros((128, 128), BF16)
    for piece in range(4):
        copies[2 * piece].wait()
        copies[2 * piece + 1].wait()
        rows = pl.ds(pl.multiple_of(place[piece] * 32, 32), 32)
        values = window[piece]
        for base, array in ((0, values), (TILES, pltpu.roll(values, 64, 1))):
            for tile in range(TILES):
                high, low = halves(array[:, 128 * tile : 128 * tile + 128])
                tiles_high[base + tile, rows, :] = high
                tiles_low[base + tile, rows, :] = low
    lower = lax.broadcasted_iota(jnp.int32, (128, 128), 1) < 64

    outs = []
    for chunk in range(2):
        for tiles, held in ((tiles_high, c_high), (tiles_low, c_low)):
            for pair in range(8):
                tile = tiles[TILES // 2 + chunk * 8 + pair]
                lanes = slice(chunk * 1024 + pair * 128, chunk * 1024 + pair * 128 + 128)
                for q in range(4):
                    held[128 * q : 128 * q + 32, lanes] = tile[32 * q : 32 * q + 32]
        for direc in range(3):
            high, low = (
                jnp.concatenate(
                    [
                        jnp.concatenate(
                            [tiles[TILES // 2 + chunk * 8 + pair] for pair in (2 * group, 2 * group + 1)]
                            + [
                                jnp.where(
                                    lower,
                                    tiles[index[direc, chunk * 16 + 2 * pair]],
                                    tiles[index[direc, chunk * 16 + 2 * pair + 1]],
                                )
                                for pair in (2 * group, 2 * group + 1)
                            ],
                            axis=1,
                        )
                        for group in range(4)
                    ],
                    axis=0,
                )
                for tiles in (tiles_high, tiles_low)
            )
            moved = product(
                jnp.concatenate([high, low, high], axis=1),
                jnp.concatenate([mats_high[direc], mats_high[direc], mats_low[direc]], axis=1),
                (1, 1),
            )
            parts = halves(moved)
            for group in range(4):
                lanes = slice(chunk * 1024 + group * 256, chunk * 1024 + group * 256 + 256)
                for q in range(4):
                    to = 128 * q + 32 * (direc + 1)
                    rows = slice(128 * group + 32 * q, 128 * group + 32 * q + 32)
                    c_high[to : to + 32, lanes] = parts[0][rows]
                    c_low[to : to + 32, lanes] = parts[1][rows]
        lanes = slice(chunk * 1024, chunk * 1024 + 1024)
        for slot, held in enumerate((c_high, c_low)):
            sem = out_sems.at[2 * chunk + slot]
            outs.append(pltpu.make_async_copy(held.at[:, lanes], cand.at[slot, :, lanes], sem))
            outs[-1].start()
        high, low = c_high[:, lanes], c_low[:, lanes]
        top = product(high[0:256], high, (1, 1))
        bottom = product(high[256:512], high[256:512], (1, 1))
        both = product(high, low, (1, 1))
        if chunk == 0:
            same[0:256, :], same[256:512, 256:512], cross[...] = top, bottom, both
        else:
            same[0:256, :] += top
            same[256:512, 256:512] += bottom
            cross[...] += both

    spot = 0
    for a in range(4):
        for b in range(a, 4):
            rows, cols = slice(128 * a, 128 * a + 128), slice(128 * b, 128 * b + 128)
            total = same[rows, cols] + (cross[rows, cols] + cross[cols, rows].T)
            total = total * (1.0 / 524288)
            to = slice(128 * spot, 128 * spot + 128)
            gram[to, :] = total if second else total + before[to, :]
            spot += 1
    for copy in outs:
        copy.wait()


def transported(second, place, index, xfactor, mains, above, before, volume, upwind):
    part = jax.ShapeDtypeStruct((2, 512, WIDE), BF16)
    extra = [] if second else [*above, before]
    return pl.pallas_call(
        functools.partial(transport_kernel, second),
        out_shape=(jax.ShapeDtypeStruct((1280, 128), F32), part),
        in_specs=[SMEM, SMEM, ANY] + [ANY] * 3 + ([] if second else [ANY] * 4 + [VMEM]) + [VMEM, VMEM],
        out_specs=(VMEM, ANY),
        scratch_shapes=[
            pltpu.VMEM((4, 32, 2 * WIDE), F32),
            pltpu.VMEM((3, 256, 512), BF16),
            pltpu.VMEM((3, 256, 512), BF16),
            pltpu.VMEM((2 * TILES + 1, 128, 128), BF16),
            pltpu.VMEM((2 * TILES + 1, 128, 128), BF16),
            pltpu.VMEM((512, WIDE), BF16),
            pltpu.VMEM((512, WIDE), BF16),
            pltpu.VMEM((512, 512), F32),
            pltpu.VMEM((512, 512), F32),
            pltpu.SemaphoreType.DMA((8,)),
            pltpu.SemaphoreType.DMA((4,)),
        ],
        compiler_params=pltpu.CompilerParams(vmem_limit_bytes=50 << 20),
        cost_estimate=pl.CostEstimate(
            flops=9_000_000_000, bytes_accessed=8 << 20, transcendentals=0
        ),
        name="transport_second" if second else "transport_first",
    )(place, index, xfactor, *mains, *extra, volume, upwind)


def along_lanes(x, lane):
    return jnp.broadcast_to(x[:, lane : lane + 1], (8, 128))


def along_rows(x, row):
    return jnp.broadcast_to(x[row : row + 1, :], (8, 128))


NEAR = 4


def factor_block(left, right):
    row = lax.broadcasted_iota(jnp.int32, (8, 128), 0)
    left, right = list(left), list(right)
    upper, inverse = [], []

    def packed(lines):
        out = lines[0]
        for j in range(1, 8):
            out = jnp.where(row == j, lines[j], out)
        return out

    for step in range(16):
        near = min(16, step + 1 + NEAR)
        c = [[along_lanes(left[i], 8 * step + l) for l in range(8)] for i in range(step, near)]
        s = [[along_rows(c[0][l], i) if i >= l else None for l in range(8)] for i in range(8)]
        lines = [[along_rows(left[step], l) for l in range(8)]]
        lines += [[along_rows(right[step], l) for l in range(8)]]
        lines += c[1:]
        for j in range(8):
            r = lax.rsqrt(s[j][j])
            for i in range(j + 1, 8):
                s[i][j] = s[i][j] * r
            for line in lines:
                line[j] = line[j] * r
            for l in range(j + 1, 8):
                for i in range(l, 8):
                    s[i][l] = s[i][l] - s[i][j] * s[l][j]
                for line in lines:
                    line[l] = line[l] - s[l][j] * line[j]
        wide_left, wide_right, *factors = lines
        upper.append(packed(wide_left))
        inverse.append(packed(wide_right))
        for i in range(step + 1, near):
            for j in range(8):
                left[i] = left[i] - factors[i - step - 1][j] * wide_left[j]
                right[i] = right[i] - factors[i - step - 1][j] * wide_right[j]
        if near < 16:
            both = jnp.concatenate([upper[-1], inverse[-1]], axis=1)
            change = exact(upper[-1][:, 8 * near :], both, (0, 0))
            for i in range(near, 16):
                rows = slice(8 * (i - near), 8 * (i - near) + 8)
                left[i] = left[i] - change[rows, :128]
                right[i] = right[i] - change[rows, 128:]
    return upper, inverse


def factor_kernel(
    place, mine, other, coeffs, cand_first, cand_second, r_out, new_out,
    packed, work, c_high, c_low, new, sems, out_sems,
):
    copies = []
    for side, cand in enumerate((cand_first, cand_second)):
        lanes = slice(side * WIDE, side * WIDE + WIDE)
        for slot, held in enumerate((c_high, c_low)):
            sem = sems.at[2 * side + slot]
            copies.append(pltpu.make_async_copy(cand.at[slot], held.at[:, lanes], sem))
    for copy in copies:
        copy.start()
    packed[pl.ds(pl.multiple_of(place[0] * 640, 640), 640), :] = mine[...]
    packed[pl.ds(pl.multiple_of((1 - place[0]) * 640, 640), 640), :] = other[...]
    row = lax.broadcasted_iota(jnp.int32, (128, 128), 0)
    col = lax.broadcasted_iota(jnp.int32, (128, 128), 1)
    eye = (row == col).astype(F32)
    zero = jnp.zeros((128, 128), F32)
    at = [slice(128 * a, 128 * a + 128) for a in range(4)]
    beside = [slice(512 + 128 * a, 640 + 128 * a) for a in range(4)]
    spot = 0
    for a in range(4):
        for b in range(4):
            work[at[a], beside[b]] = eye if a == b else zero
            if b >= a:
                work[at[a], at[b]] = packed[128 * spot : 128 * spot + 128, :]
                spot += 1
            else:
                r_out[at[a], at[b]] = zero
    for a in range(4):
        first = 128 * a
        upper, inverse = factor_block(
            [work[first + 8 * i : first + 8 * i + 8, at[a]] for i in range(16)],
            [eye[8 * i : 8 * i + 8] for i in range(16)],
        )
        diag = jnp.where(row >= col, jnp.concatenate(inverse, axis=0), 0.0)
        r_out[at[a], at[a]] = jnp.where(row <= col, jnp.concatenate(upper, axis=0), 0.0)
        work[at[a], beside[a]] = diag
        if a:
            done = slice(512, 512 + first)
            work[at[a], done] = exact(diag, work[at[a], done], (1, 0))
        if a < 3:
            rest = exact(diag, work[at[a], first + 128 : 512], (1, 0))
            r_out[at[a], first + 128 : 512] = rest
            for b in range(a + 1, 4):
                part = rest[:, 128 * (b - a - 1) : 128 * (b - a)]
                right = slice(128 * b, 512)
                work[at[b], right] -= exact(part, rest[:, 128 * (b - a - 1) :], (0, 0))
                done = slice(512, 512 + first + 128)
                work[at[b], done] -= exact(part, work[at[a], done], (0, 0))
    weight_high, weight_low = halves(exact(coeffs[...], work[:, 512:1024], (0, 0)))
    for copy in copies:
        copy.wait()
    outs = []
    for chunk in range(4):
        lanes = slice(chunk * 1024, chunk * 1024 + 1024)
        high, low = c_high[:, lanes], c_low[:, lanes]
        new[:, lanes] = product(weight_high, high, (1, 0)) + (
            product(weight_high, low, (1, 0)) + product(weight_low, high, (1, 0))
        )
        outs.append(pltpu.make_async_copy(new.at[:, lanes], new_out.at[:, lanes], out_sems.at[chunk]))
        outs[-1].start()
    for copy in outs:
        copy.wait()


def factored(place, mine, other, coeffs, cand_first, cand_second):
    return pl.pallas_call(
        factor_kernel,
        out_shape=(
            jax.ShapeDtypeStruct((512, 512), F32),
            jax.ShapeDtypeStruct((128, 2 * WIDE), F32),
        ),
        in_specs=[SMEM, VMEM, VMEM, VMEM, ANY, ANY],
        out_specs=(VMEM, ANY),
        scratch_shapes=[
            pltpu.VMEM((1280, 128), F32),
            pltpu.VMEM((512, 1024), F32),
            pltpu.VMEM((512, 2 * WIDE), BF16),
            pltpu.VMEM((512, 2 * WIDE), BF16),
            pltpu.VMEM((128, 2 * WIDE), F32),
            pltpu.SemaphoreType.DMA((4,)),
            pltpu.SemaphoreType.DMA((4,)),
        ],
        compiler_params=pltpu.CompilerParams(vmem_limit_bytes=52 << 20),
        name="factor",
    )(place, mine, other, coeffs, cand_first, cand_second)


def sent(value, axis, by):
    count = lax.axis_size(axis)
    return lax.ppermute(value, axis, [(i, (i + by) % count) for i in range(count)])


def pieces_from_here(value, axis):
    count, here = lax.axis_size(axis), lax.axis_index(axis)
    split = value.reshape(count, -1, value.shape[-1])
    return [
        lax.dynamic_index_in_dim(split, (here + by) % count, 0, keepdims=False)
        for by in range(count)
    ]


def scattered_sum(value, axis):
    pieces = pieces_from_here(value, axis)
    return sum((sent(pieces[by], axis, by) for by in range(1, len(pieces))), pieces[0])


def exchanged_sum(value, axis):
    one, two, three = (sent(value, axis, by) for by in range(1, 4))
    return (value + two) + (one + three)


def gathered(value, axis):
    count, here = lax.axis_size(axis), lax.axis_index(axis)
    out = jnp.zeros((count, *value.shape), value.dtype)
    for by in range(count):
        part = sent(value, axis, by) if by else value
        out = lax.dynamic_update_index_in_dim(out, part, (here - by) % count, 0)
    return out.reshape(-1, value.shape[-1])


def summed(gram):
    part = scattered_sum(scattered_sum(gram, "core"), "x")
    part = exchanged_sum(exchanged_sum(part, "y"), "rank")
    mine = gathered(part, "x")
    return mine, sent(mine, "core", 1)


def tile_index(neighbor, first):
    at = neighbor - first
    odd_place = jnp.arange(neighbor.shape[1]) % 2
    tile = jnp.where(at % 2 == odd_place, at // 2, TILES + (at + 1) // 2)
    return jnp.where(neighbor >= 0, tile, ZERO_TILE).astype(jnp.int32)


def shards(xfactor, volume, upwind, neighbor, coeffs):
    sub_elems = neighbor.shape[1] // 4
    rank = lax.axis_index("rank")
    count = lax.axis_size(SPACE)
    above = xfactor[:, 7 * WIDE :]
    above = lax.ppermute(above, SPACE, [(i, i + 1) for i in range(count - 1)])
    mains, halos = [], []
    for by in range(1, 4):
        to = (rank + by) % 4
        piece = lax.dynamic_slice_in_dim(xfactor, to * 2 * WIDE, 2 * WIDE, 1)
        mains.append(sent(piece, "rank", by))
    for by in range(4):
        to = (rank + by) % 4
        inside = lax.dynamic_slice_in_dim(xfactor, jnp.maximum((2 * to - 1) * WIDE, 0), WIDE, 1)
        piece = jnp.where(to == 0, above, inside)
        halos.append(sent(piece, "rank", by) if by else piece)
    place = jnp.stack([(rank - by) % 4 for by in range(4)]).astype(jnp.int32)
    first = (lax.axis_index(SPACE) * 4 + rank) * sub_elems
    own = lax.dynamic_slice_in_dim(neighbor, rank * sub_elems, sub_elems, 1)
    index_first = tile_index(own[:, :HALO_EL], first - HALO_EL)
    index_second = tile_index(own[:, HALO_EL:], first)
    before, second = transported(
        True, place, index_second, xfactor, mains, None, None, volume, upwind
    )
    gram, start = transported(
        False, place, index_first, xfactor, mains, halos, before, volume, upwind
    )
    mine, other = summed(gram)
    core = lax.axis_index("core").astype(jnp.int32).reshape(1)
    r_factor, new_factor = factored(core, mine, other, coeffs, start, second)
    return new_factor, r_factor


def solution(mesh):
    finer = Mesh(mesh.devices.reshape(4, 4, 2, 4), SPACE_RANK)
    placed = (P("rank", SPACE), P(), P(), P(None, SPACE), P())
    return jax.shard_map(
        shards, mesh=finer, in_specs=placed, out_specs=(P(None, SPACE_RANK), P()), check_vma=False
    )
```

profile of v0, /device:TPU:1, one launch (start us, length us, event | category | flops | bytes accessed | tf_op | source)
XLA Modules:
  0.0 117.3 jit_solution(9889671113541861938)
XLA Ops:
  2.2 2.5 %collective-permute-start = (f32[32,4096]{1,0:T(8,128)S(1)}, f32[32,4096]{1,0:T(8,128)S(1)}, u32[]{:S(2)}, u32[]{:S(2)}) collective-permute-start(f32[32,4096]{1,0:T(8,128)S(1)} %get-tuple-element.22), channel_id=1, source_target_pairs={{0,1},{1,2},{2,3},{3,0},{4,5},{5,6},{6,7},{7,4},{8,9},{9,10},{10,1... | collective-permute-start | bytes 1572872 | tf_op jit(solution)/shard_map/ppermute | solution.py:341
  4.7 3.3 %collective-permute-start.1 = (f32[32,4096]{1,0:T(8,128)S(1)}, f32[32,4096]{1,0:T(8,128)S(1)}, u32[]{:S(2)}, u32[]{:S(2)}) collective-permute-start(f32[32,4096]{1,0:T(8,128)S(1)} %get-tuple-element.21), channel_id=1, source_target_pairs={{0,2},{1,3},{2,0},{3,1},{4,6},{5,7},{6,4},{7,5},{8,10},{9,11},{10,... | collective-permute-start | bytes 1572872 | tf_op jit(solution)/shard_map/ppermute | solution.py:341
  8.8 1.7 %slice.10 = f32[32,2048]{1,0:T(8,128)} slice(f32[32,16384]{1,0:T(8,128)} %xfactor.3), slice={[0:32], [14336:16384]} | slice | bytes 524288 | tf_op jit(solution)/shard_map/slice | solution.py:390
  10.4 4.6 %collective-permute-start.3 = (f32[32,2048]{1,0:T(8,128)}, f32[32,2048]{1,0:T(8,128)}, u32[]{:S(2)}, u32[]{:S(2)}) collective-permute-start(f32[32,2048]{1,0:T(8,128)} %slice.10), channel_id=1, source_target_pairs={{0,4},{4,8},{8,12},{12,16},{16,20},{20,24},{24,28},{28,32},{32,36}... | collective-permute-start | bytes 786440 | tf_op jit(solution)/shard_map/ppermute | solution.py:391
  15.4 3.2 %collective-permute-done.3 = f32[32,2048]{1,0:T(8,128)} collective-permute-done((f32[32,2048]{1,0:T(8,128)}, f32[32,2048]{1,0:T(8,128)}, u32[]{:S(2)}, u32[]{:S(2)}) %collective-permute-start.3) | collective-permute-done | bytes 262176 | tf_op jit(solution)/shard_map/ppermute | solution.py:391
  21.2 2.3 %collective-permute-start.6 = (f32[32,2048]{1,0:T(8,128)S(1)}, f32[32,2048]{1,0:T(8,128)S(1)}, u32[]{:S(2)}, u32[]{:S(2)}) collective-permute-start(f32[32,2048]{1,0:T(8,128)S(1)} %get-tuple-element.16), channel_id=1, source_target_pairs={{0,3},{1,0},{2,1},{3,2},{4,7},{5,4},{6,5},{7,6},{8,11},{9,8},{10,9... | collective-permute-start | bytes 786440 | tf_op jit(solution)/shard_map/ppermute | solution.py:341
  23.6 7.1 %collective-permute-done.1.refs_1_ = f32[32,4096]{1,0:T(8,128)S(1)} collective-permute-done((f32[32,4096]{1,0:T(8,128)S(1)}, f32[32,4096]{1,0:T(8,128)S(1)}, u32[]{:S(2)}, u32[]{:S(2)}) %collective-permute-start.1) | collective-permute-done | bytes 524320 | tf_op jit(solution)/shard_map/ppermute | solution.py:341
  30.6 8.4 %transport_second.1 = (f32[1280,128]{1,0:T(8,128)S(1)}, bf16[2,512,2048]{2,1,0:T(8,128)(2,1)}) custom-call(s32[4]{0:T(128)S(1)} %pad_add_fusion.place, s32[3,32]{1,0:T(4,128)S(1)} %get-tuple-element.26.index, f32[32,16384]{1,0:T(8,128)} %xfactor.3, f32[32,4096]{1,0:T(8,128)S(1)} %collective-permute-done.refs_0_, ...), custom_call_target="tpu_custom_call" | custom-call | flops 8999999488 | bytes 8388608 | tf_op jit(solution)/shard_map/transport_second/pallas_call | solution.py:167
  39.9 2.0 %collective-permute-done.5.refs_5_ = f32[32,2048]{1,0:T(8,128)S(1)} collective-permute-done((f32[32,2048]{1,0:T(8,128)S(1)}, f32[32,2048]{1,0:T(8,128)S(1)}, u32[]{:S(2)}, u32[]{:S(2)}) %collective-permute-start.5) | collective-permute-done | bytes 262176 | tf_op jit(solution)/shard_map/ppermute | solution.py:341
  41.9 8.8 %transport_first.1 = (f32[1280,128]{1,0:T(8,128)S(1)}, bf16[2,512,2048]{2,1,0:T(8,128)(2,1)}) custom-call(s32[4]{0:T(128)S(1)} %pad_add_fusion.place, s32[3,32]{1,0:T(4,128)S(1)} %get-tuple-element.27.index, f32[32,16384]{1,0:T(8,128)} %xfactor.3, f32[32,4096]{1,0:T(8,128)S(1)} %collective-permute-done.refs_0_, ...), custom_call_target="tpu_custom_call" | custom-call | flops 8999999488 | bytes 8388608 | tf_op jit(solution)/shard_map/transport_first/pallas_call | solution.py:167
  53.7 2.5 %collective-permute-start.10 = (f32[160,128]{1,0:T(8,128)S(1)}, f32[160,128]{1,0:T(8,128)S(1)}, u32[]{:S(2)}, u32[]{:S(2)}) collective-permute-start(f32[160,128]{1,0:T(8,128)S(1)} %get-tuple-element.24), channel_id=1, source_target_pairs={{0,96},{32,0},{64,32},{96,64},{1,97},{33,1},{65,33},{97,65},{2,98}... | collective-permute-start | bytes 245768 | tf_op jit(solution)/shard_map/ppermute | solution.py:341
  56.3 1.7 %collective-permute-start.9 = (f32[160,128]{1,0:T(8,128)S(1)}, f32[160,128]{1,0:T(8,128)S(1)}, u32[]{:S(2)}, u32[]{:S(2)}) collective-permute-start(f32[160,128]{1,0:T(8,128)S(1)} %get-tuple-element.25), channel_id=1, source_target_pairs={{0,64},{32,96},{64,0},{96,32},{1,65},{33,97},{65,1},{97,33},{2,66}... | collective-permute-start | bytes 245768 | tf_op jit(solution)/shard_map/ppermute | solution.py:341
  58.0 4.0 %collective-permute-done.8 = f32[160,128]{1,0:T(8,128)S(1)} collective-permute-done((f32[160,128]{1,0:T(8,128)S(1)}, f32[160,128]{1,0:T(8,128)S(1)}, u32[]{:S(2)}, u32[]{:S(2)}) %collective-permute-start.8) | collective-permute-done | bytes 81952 | tf_op jit(solution)/shard_map/ppermute | solution.py:341
  62.3 3.0 %collective-permute-start.11 = (f32[160,128]{1,0:T(8,128)S(1)}, f32[160,128]{1,0:T(8,128)S(1)}, u32[]{:S(2)}, u32[]{:S(2)}) collective-permute-start(f32[160,128]{1,0:T(8,128)S(1)} %fusion.1), channel_id=1, source_target_pairs={{0,16},{8,24},{16,0},{24,8},{1,17},{9,25},{17,1},{25,9},{2,18},{10... | collective-permute-start | bytes 245768 | tf_op jit(solution)/shard_map/ppermute | solution.py:341
  65.7 2.3 %collective-permute-start.13 = (f32[160,128]{1,0:T(8,128)S(1)}, f32[160,128]{1,0:T(8,128)S(1)}, u32[]{:S(2)}, u32[]{:S(2)}) collective-permute-start(f32[160,128]{1,0:T(8,128)S(1)} %fusion.1), channel_id=1, source_target_pairs={{0,24},{8,0},{16,8},{24,16},{1,25},{9,1},{17,9},{25,17},{2,26},{10... | collective-permute-start | bytes 245768 | tf_op jit(solution)/shard_map/ppermute | solution.py:341
  67.9 2.5 %collective-permute-done.12 = f32[160,128]{1,0:T(8,128)S(1)} collective-permute-done((f32[160,128]{1,0:T(8,128)S(1)}, f32[160,128]{1,0:T(8,128)S(1)}, u32[]{:S(2)}, u32[]{:S(2)}) %collective-permute-start.12) | collective-permute-done | bytes 81952 | tf_op jit(solution)/shard_map/ppermute | solution.py:341
  70.5 2.0 %collective-permute-start.14 = (f32[160,128]{1,0:T(8,128)S(1)}, f32[160,128]{1,0:T(8,128)S(1)}, u32[]{:S(2)}, u32[]{:S(2)}) collective-permute-start(f32[160,128]{1,0:T(8,128)S(1)} %add_add_fusion.1), channel_id=1, source_target_pairs={{0,2},{1,3},{2,0},{3,1},{4,6},{5,7},{6,4},{7,5},{8,10},{9,11},{10,... | collective-permute-start | bytes 245768 | tf_op jit(solution)/shard_map/ppermute | solution.py:341
  72.5 1.7 %collective-permute-start.15 = (f32[160,128]{1,0:T(8,128)S(1)}, f32[160,128]{1,0:T(8,128)S(1)}, u32[]{:S(2)}, u32[]{:S(2)}) collective-permute-start(f32[160,128]{1,0:T(8,128)S(1)} %add_add_fusion.1), channel_id=1, source_target_pairs={{0,1},{1,2},{2,3},{3,0},{4,5},{5,6},{6,7},{7,4},{8,9},{9,10},{10,1... | collective-permute-start | bytes 245768 | tf_op jit(solution)/shard_map/ppermute | solution.py:341
  74.2 2.3 %collective-permute-start.16 = (f32[160,128]{1,0:T(8,128)S(1)}, f32[160,128]{1,0:T(8,128)S(1)}, u32[]{:S(2)}, u32[]{:S(2)}) collective-permute-start(f32[160,128]{1,0:T(8,128)S(1)} %add_add_fusion.1), channel_id=1, source_target_pairs={{0,3},{1,0},{2,1},{3,2},{4,7},{5,4},{6,5},{7,6},{8,11},{9,8},{10,9... | collective-permute-start | bytes 245768 | tf_op jit(solution)/shard_map/ppermute | solution.py:341
  76.6 2.7 %collective-permute-done.15 = f32[160,128]{1,0:T(8,128)S(1)} collective-permute-done((f32[160,128]{1,0:T(8,128)S(1)}, f32[160,128]{1,0:T(8,128)S(1)}, u32[]{:S(2)}, u32[]{:S(2)}) %collective-permute-start.15) | collective-permute-done | bytes 81952 | tf_op jit(solution)/shard_map/ppermute | solution.py:341
  79.5 2.7 %collective-permute-start.18 = (f32[160,128]{1,0:T(8,128)S(1)}, f32[160,128]{1,0:T(8,128)S(1)}, u32[]{:S(2)}, u32[]{:S(2)}) collective-permute-start(f32[160,128]{1,0:T(8,128)S(1)} %get-tuple-element.15), channel_id=1, source_target_pairs={{0,64},{32,96},{64,0},{96,32},{1,65},{33,97},{65,1},{97,33},{2,66}... | collective-permute-start | bytes 245768 | tf_op jit(solution)/shard_map/ppermute | solution.py:341
  82.2 1.7 %collective-permute-done.17 = f32[160,128]{1,0:T(8,128)S(1)} collective-permute-done((f32[160,128]{1,0:T(8,128)S(1)}, f32[160,128]{1,0:T(8,128)S(1)}, u32[]{:S(2)}, u32[]{:S(2)}) %collective-permute-start.17) | collective-permute-done | bytes 81952 | tf_op jit(solution)/shard_map/ppermute | solution.py:341
  85.5 5.0 %collective-permute-start.20 = (f32[640,128]{1,0:T(8,128)S(1)}, f32[640,128]{1,0:T(8,128)S(1)}, u32[]{:S(2)}, u32[]{:S(2)}) collective-permute-start(f32[640,128]{1,0:T(8,128)S(1)} %bitcast.32), channel_id=1, source_target_pairs={{0,4},{4,0},{1,5},{5,1},{2,6},{6,2},{3,7},{7,3},{8,12},{12,8},{9,1... | collective-permute-start | bytes 983048 | tf_op jit(solution)/shard_map/ppermute | solution.py:341
  91.8 25.3 %factor.1 = (f32[512,512]{1,0:T(8,128)}, f32[128,4096]{1,0:T(8,128)}) custom-call(s32[1]{0:T(128)} %bitcast.place, f32[640,128]{1,0:T(8,128)S(1)} %bitcast.33, f32[640,128]{1,0:T(8,128)S(1)} %collective-permute-done.20.other, f32[512,128]{1,0:T(8,128)S(1)} %copy-done.1, bf16[2,512,2048]{2,1,0:T(8,128)(2,1)} %get-tuple-element.10.cand_first, ...), custom_call_target="tpu_custom_call" | custom-call | tf_op jit(solution)/shard_map/factor/pallas_call | solution.py:317
  (48 shorter events, 12.6 us)
Async XLA Ops:
  2.2 28.5 %copy-start.2 = (f32[3,64,64]{2,1,0:T(8,128)S(1)}, f32[3,64,64]{2,1,0:T(8,128)}, u32[]{:S(2)}) copy-start(f32[3,64,64]{2,1,0:T(8,128)} %refs_8_.1) | copy-start | bytes 147460
  2.2 28.5 %copy-start.3 = (f32[3,64,64]{2,1,0:T(8,128)S(1)}, f32[3,64,64]{2,1,0:T(8,128)}, u32[]{:S(2)}) copy-start(f32[3,64,64]{2,1,0:T(8,128)} %refs_9_.1) | copy-start | bytes 147460
  2.2 19.1 %collective-permute-start = (f32[32,4096]{1,0:T(8,128)S(1)}, f32[32,4096]{1,0:T(8,128)S(1)}, u32[]{:S(2)}, u32[]{:S(2)}) collective-permute-start(f32[32,4096]{1,0:T(8,128)S(1)} %get-tuple-element.22), channel_id=1, source_target_pairs={{0,1},{1,2},{2,3},{3,0},{4,5},{5,6},{6,7},{7,4},{8,9},{9,10},{10,1... | collective-permute-start | bytes 1572872 | tf_op jit(solution)/shard_map/ppermute | solution.py:341
  4.7 25.9 %collective-permute-start.1 = (f32[32,4096]{1,0:T(8,128)S(1)}, f32[32,4096]{1,0:T(8,128)S(1)}, u32[]{:S(2)}, u32[]{:S(2)}) collective-permute-start(f32[32,4096]{1,0:T(8,128)S(1)} %get-tuple-element.21), channel_id=1, source_target_pairs={{0,2},{1,3},{2,0},{3,1},{4,6},{5,7},{6,4},{7,5},{8,10},{9,11},{10,... | collective-permute-start | bytes 1572872 | tf_op jit(solution)/shard_map/ppermute | solution.py:341
  8.0 22.6 %collective-permute-start.2 = (f32[32,4096]{1,0:T(8,128)S(1)}, f32[32,4096]{1,0:T(8,128)S(1)}, u32[]{:S(2)}, u32[]{:S(2)}) collective-permute-start(f32[32,4096]{1,0:T(8,128)S(1)} %get-tuple-element.20), channel_id=1, source_target_pairs={{0,3},{1,0},{2,1},{3,2},{4,7},{5,4},{6,5},{7,6},{8,11},{9,8},{10,9... | collective-permute-start | bytes 1572872 | tf_op jit(solution)/shard_map/ppermute | solution.py:341
  10.4 8.2 %collective-permute-start.3 = (f32[32,2048]{1,0:T(8,128)}, f32[32,2048]{1,0:T(8,128)}, u32[]{:S(2)}, u32[]{:S(2)}) collective-permute-start(f32[32,2048]{1,0:T(8,128)} %slice.10), channel_id=1, source_target_pairs={{0,4},{4,8},{8,12},{12,16},{16,20},{20,24},{24,28},{28,32},{32,36}... | collective-permute-start | bytes 786440 | tf_op jit(solution)/shard_map/ppermute | solution.py:391
  20.3 19.6 %collective-permute-start.4 = (f32[32,2048]{1,0:T(8,128)S(1)}, f32[32,2048]{1,0:T(8,128)S(1)}, u32[]{:S(2)}, u32[]{:S(2)}) collective-permute-start(f32[32,2048]{1,0:T(8,128)S(1)} %get-tuple-element.18), channel_id=1, source_target_pairs={{0,1},{1,2},{2,3},{3,0},{4,5},{5,6},{6,7},{7,4},{8,9},{9,10},{10,1... | collective-permute-start | bytes 786440 | tf_op jit(solution)/shard_map/ppermute | solution.py:341
  21.1 20.8 %collective-permute-start.5 = (f32[32,2048]{1,0:T(8,128)S(1)}, f32[32,2048]{1,0:T(8,128)S(1)}, u32[]{:S(2)}, u32[]{:S(2)}) collective-permute-start(f32[32,2048]{1,0:T(8,128)S(1)} %get-tuple-element.17), channel_id=1, source_target_pairs={{0,2},{1,3},{2,0},{3,1},{4,6},{5,7},{6,4},{7,5},{8,10},{9,11},{10,... | collective-permute-start | bytes 786440 | tf_op jit(solution)/shard_map/ppermute | solution.py:341
  21.2 20.6 %collective-permute-start.6 = (f32[32,2048]{1,0:T(8,128)S(1)}, f32[32,2048]{1,0:T(8,128)S(1)}, u32[]{:S(2)}, u32[]{:S(2)}) collective-permute-start(f32[32,2048]{1,0:T(8,128)S(1)} %get-tuple-element.16), channel_id=1, source_target_pairs={{0,3},{1,0},{2,1},{3,2},{4,7},{5,4},{6,5},{7,6},{8,11},{9,8},{10,9... | collective-permute-start | bytes 786440 | tf_op jit(solution)/shard_map/ppermute | solution.py:341
  50.7 41.1 %copy-start.1 = (f32[512,128]{1,0:T(8,128)S(1)}, f32[512,128]{1,0:T(8,128)}, u32[]{:S(2)}) copy-start(f32[512,128]{1,0:T(8,128)} %coeffs.1) | copy-start | bytes 786436
  50.8 2.9 %collective-permute-start.7 = (f32[640,128]{1,0:T(8,128)S(1)}, f32[640,128]{1,0:T(8,128)S(1)}, u32[]{:S(2)}, u32[]{:S(2)}) collective-permute-start(f32[640,128]{1,0:T(8,128)S(1)} %dynamic-slice_bitcast_fusion), channel_id=1, source_target_pairs={{0,4},{4,0},{1,5},{5,1},{2,6},{6,2},{3,7},{7,3},{8,12},{12,8},{9,1... | collective-permute-start | bytes 983048 | tf_op jit(solution)/shard_map/ppermute | solution.py:341
  53.7 4.3 %collective-permute-start.10 = (f32[160,128]{1,0:T(8,128)S(1)}, f32[160,128]{1,0:T(8,128)S(1)}, u32[]{:S(2)}, u32[]{:S(2)}) collective-permute-start(f32[160,128]{1,0:T(8,128)S(1)} %get-tuple-element.24), channel_id=1, source_target_pairs={{0,96},{32,0},{64,32},{96,64},{1,97},{33,1},{65,33},{97,65},{2,98}... | collective-permute-start | bytes 245768 | tf_op jit(solution)/shard_map/ppermute | solution.py:341
  56.3 5.7 %collective-permute-start.8 = (f32[160,128]{1,0:T(8,128)S(1)}, f32[160,128]{1,0:T(8,128)S(1)}, u32[]{:S(2)}, u32[]{:S(2)}) collective-permute-start(f32[160,128]{1,0:T(8,128)S(1)} %get-tuple-element.23), channel_id=1, source_target_pairs={{0,32},{32,64},{64,96},{96,0},{1,33},{33,65},{65,97},{97,1},{2,34}... | collective-permute-start | bytes 245768 | tf_op jit(solution)/shard_map/ppermute | solution.py:341
  56.3 6.0 %collective-permute-start.9 = (f32[160,128]{1,0:T(8,128)S(1)}, f32[160,128]{1,0:T(8,128)S(1)}, u32[]{:S(2)}, u32[]{:S(2)}) collective-permute-start(f32[160,128]{1,0:T(8,128)S(1)} %get-tuple-element.25), channel_id=1, source_target_pairs={{0,64},{32,96},{64,0},{96,32},{1,65},{33,97},{65,1},{97,33},{2,66}... | collective-permute-start | bytes 245768 | tf_op jit(solution)/shard_map/ppermute | solution.py:341
  62.3 5.7 %collective-permute-start.11 = (f32[160,128]{1,0:T(8,128)S(1)}, f32[160,128]{1,0:T(8,128)S(1)}, u32[]{:S(2)}, u32[]{:S(2)}) collective-permute-start(f32[160,128]{1,0:T(8,128)S(1)} %fusion.1), channel_id=1, source_target_pairs={{0,16},{8,24},{16,0},{24,8},{1,17},{9,25},{17,1},{25,9},{2,18},{10... | collective-permute-start | bytes 245768 | tf_op jit(solution)/shard_map/ppermute | solution.py:341
  65.3 5.2 %collective-permute-start.12 = (f32[160,128]{1,0:T(8,128)S(1)}, f32[160,128]{1,0:T(8,128)S(1)}, u32[]{:S(2)}, u32[]{:S(2)}) collective-permute-start(f32[160,128]{1,0:T(8,128)S(1)} %fusion.1), channel_id=1, source_target_pairs={{0,8},{8,16},{16,24},{24,0},{1,9},{9,17},{17,25},{25,1},{2,10},{10... | collective-permute-start | bytes 245768 | tf_op jit(solution)/shard_map/ppermute | solution.py:341
  65.7 4.8 %collective-permute-start.13 = (f32[160,128]{1,0:T(8,128)S(1)}, f32[160,128]{1,0:T(8,128)S(1)}, u32[]{:S(2)}, u32[]{:S(2)}) collective-permute-start(f32[160,128]{1,0:T(8,128)S(1)} %fusion.1), channel_id=1, source_target_pairs={{0,24},{8,0},{16,8},{24,16},{1,25},{9,1},{17,9},{25,17},{2,26},{10... | collective-permute-start | bytes 245768 | tf_op jit(solution)/shard_map/ppermute | solution.py:341
  70.5 6.1 %collective-permute-start.14 = (f32[160,128]{1,0:T(8,128)S(1)}, f32[160,128]{1,0:T(8,128)S(1)}, u32[]{:S(2)}, u32[]{:S(2)}) collective-permute-start(f32[160,128]{1,0:T(8,128)S(1)} %add_add_fusion.1), channel_id=1, source_target_pairs={{0,2},{1,3},{2,0},{3,1},{4,6},{5,7},{6,4},{7,5},{8,10},{9,11},{10,... | collective-permute-start | bytes 245768 | tf_op jit(solution)/shard_map/ppermute | solution.py:341
  72.5 6.8 %collective-permute-start.15 = (f32[160,128]{1,0:T(8,128)S(1)}, f32[160,128]{1,0:T(8,128)S(1)}, u32[]{:S(2)}, u32[]{:S(2)}) collective-permute-start(f32[160,128]{1,0:T(8,128)S(1)} %add_add_fusion.1), channel_id=1, source_target_pairs={{0,1},{1,2},{2,3},{3,0},{4,5},{5,6},{6,7},{7,4},{8,9},{9,10},{10,1... | collective-permute-start | bytes 245768 | tf_op jit(solution)/shard_map/ppermute | solution.py:341
  74.2 5.0 %collective-permute-start.16 = (f32[160,128]{1,0:T(8,128)S(1)}, f32[160,128]{1,0:T(8,128)S(1)}, u32[]{:S(2)}, u32[]{:S(2)}) collective-permute-start(f32[160,128]{1,0:T(8,128)S(1)} %add_add_fusion.1), channel_id=1, source_target_pairs={{0,3},{1,0},{2,1},{3,2},{4,7},{5,4},{6,5},{7,6},{8,11},{9,8},{10,9... | collective-permute-start | bytes 245768 | tf_op jit(solution)/shard_map/ppermute | solution.py:341
  79.3 4.6 %collective-permute-start.17 = (f32[160,128]{1,0:T(8,128)S(1)}, f32[160,128]{1,0:T(8,128)S(1)}, u32[]{:S(2)}, u32[]{:S(2)}) collective-permute-start(f32[160,128]{1,0:T(8,128)S(1)} %get-tuple-element.15), channel_id=1, source_target_pairs={{0,32},{32,64},{64,96},{96,0},{1,33},{33,65},{65,97},{97,1},{2,34}... | collective-permute-start | bytes 245768 | tf_op jit(solution)/shard_map/ppermute | solution.py:341
  79.5 5.4 %collective-permute-start.18 = (f32[160,128]{1,0:T(8,128)S(1)}, f32[160,128]{1,0:T(8,128)S(1)}, u32[]{:S(2)}, u32[]{:S(2)}) collective-permute-start(f32[160,128]{1,0:T(8,128)S(1)} %get-tuple-element.15), channel_id=1, source_target_pairs={{0,64},{32,96},{64,0},{96,32},{1,65},{33,97},{65,1},{97,33},{2,66}... | collective-permute-start | bytes 245768 | tf_op jit(solution)/shard_map/ppermute | solution.py:341
  82.2 3.3 %collective-permute-start.19 = (f32[160,128]{1,0:T(8,128)S(1)}, f32[160,128]{1,0:T(8,128)S(1)}, u32[]{:S(2)}, u32[]{:S(2)}) collective-permute-start(f32[160,128]{1,0:T(8,128)S(1)} %get-tuple-element.15), channel_id=1, source_target_pairs={{0,96},{32,0},{64,32},{96,64},{1,97},{33,1},{65,33},{97,65},{2,98}... | collective-permute-start | bytes 245768 | tf_op jit(solution)/shard_map/ppermute | solution.py:341
  85.5 6.3 %collective-permute-start.20 = (f32[640,128]{1,0:T(8,128)S(1)}, f32[640,128]{1,0:T(8,128)S(1)}, u32[]{:S(2)}, u32[]{:S(2)}) collective-permute-start(f32[640,128]{1,0:T(8,128)S(1)} %bitcast.32), channel_id=1, source_target_pairs={{0,4},{4,0},{1,5},{5,1},{2,6},{6,2},{3,7},{7,3},{8,12},{12,8},{9,1... | collective-permute-start | bytes 983048 | tf_op jit(solution)/shard_map/ppermute | solution.py:341
  (2 other events, 15.4 us)
where the time goes:
time: 118 us; the launch traced here: 117 us
  Pallas kernels  42.5 us (36%)
  starting transfers between devices  39.9 us (34%)
  waiting for transfers between devices  27.5 us (23%)
  local copies, waits for them, and re-layouts  4.18 us (4%)
  other arithmetic  1.89 us (2%)
  between operations  1.24 us (1%)
    ppermute x20, starting transfers between devices, sent(): lax.ppermute(value, axis, [(i, (i + by) % count) for i in range(count)])  35.3 us
    pallas_call x1, Pallas kernels, factored(): pl.pallas_call(factor_kernel, out_shape=(jax.ShapeDtypeStruct((512, 512),...  25.3 us
    ppermute x20, waiting for transfers between devices, sent(): lax.ppermute(value, axis, [(i, (i + by) % count) for i in range(count)])  24.3 us
    pallas_call x2, Pallas kernels, transported(): pl.pallas_call(functools.partial(transport_kernel, second), out_shape=(ja...  17.2 us
    ppermute x1, starting transfers between devices, shards(): above = lax.ppermute(above, SPACE, [(i, i + 1) for i in range(count - 1)])  4.59 us
    ppermute x1, waiting for transfers between devices, shards(): above = lax.ppermute(above, SPACE, [(i, i + 1) for i in range(count - 1)])  3.24 us
  transfers between devices with their start and end apart: 21, of which 12 were waited for; matrix products, arithmetic and copies ran while one was open for 3% of the time, Pallas kernels for 7%

commit v1 on v0

--- a/solution.py
+++ b/solution.py
@@ -43,9 +43,10 @@
     mains, refs = refs[:3], refs[3:]
     above, refs = ((), refs) if second else (refs[:4], refs[4:])
     before, refs = (None, refs) if second else (refs[0], refs[1:])
-    volume, upwind, gram, cand = refs[:4]
-    window, mats_high, mats_low, tiles_high, tiles_low = refs[4:9]
-    c_high, c_low, same, cross, in_sems, out_sems = refs[9:]
+    volume, upwind, *refs = refs
+    grams, refs = (refs[:1], refs[1:]) if second else (refs[:2], refs[2:])
+    cand, window, mats_high, mats_low, tiles_high, tiles_low = refs[:6]
+    c_high, c_low, same, cross, packed, added, in_sems, out_sems = refs[6:]
 
     copies = []
     own = pl.multiple_of(place[0] * 2 * WIDE, 2 * WIDE)
@@ -59,6 +60,8 @@
         for side in range(2):
             to = window.at[piece, :, side * WIDE : side * WIDE + WIDE]
             copies.append(pltpu.make_async_copy(sources[side], to, in_sems.at[2 * piece + side]))
+    if not second:
+        copies.append(pltpu.make_async_copy(before, added, in_sems.at[8]))
     for copy in copies:
         copy.start()
 
@@ -148,6 +151,8 @@
             same[256:512, 256:512] += bottom
             cross[...] += both
 
+    if not second:
+        copies[8].wait()
     spot = 0
     for a in range(4):
         for b in range(a, 4):
@@ -155,8 +160,15 @@
             total = same[rows, cols] + (cross[rows, cols] + cross[cols, rows].T)
             total = total * (1.0 / 524288)
             to = slice(128 * spot, 128 * spot + 128)
-            gram[to, :] = total if second else total + before[to, :]
+            packed[to, :] = total if second else total + added[to, :]
             spot += 1
+    if second:
+        outs.append(pltpu.make_async_copy(packed, grams[0], out_sems.at[4]))
+        outs[-1].start()
+    else:
+        for half in range(2):
+            core = place[4] if half == 0 else 1 - place[4]
+            grams[half][...] = packed[pl.ds(pl.multiple_of(core * 640, 640), 640), :]
     for copy in outs:
         copy.wait()
 
@@ -164,11 +176,13 @@
 def transported(second, place, index, xfactor, mains, above, before, volume, upwind):
     part = jax.ShapeDtypeStruct((2, 512, WIDE), BF16)
     extra = [] if second else [*above, before]
+    shapes = [(1280, 128)] if second else [(640, 128), (640, 128)]
+    grams = [jax.ShapeDtypeStruct(shape, F32) for shape in shapes]
     return pl.pallas_call(
         functools.partial(transport_kernel, second),
-        out_shape=(jax.ShapeDtypeStruct((1280, 128), F32), part),
-        in_specs=[SMEM, SMEM, ANY] + [ANY] * 3 + ([] if second else [ANY] * 4 + [VMEM]) + [VMEM, VMEM],
-        out_specs=(VMEM, ANY),
+        out_shape=(*grams, part),
+        in_specs=[SMEM, SMEM, ANY] + [ANY] * 3 + ([] if second else [ANY] * 5) + [VMEM, VMEM],
+        out_specs=(ANY, ANY) if second else (VMEM, VMEM, ANY),
         scratch_shapes=[
             pltpu.VMEM((4, 32, 2 * WIDE), F32),
             pltpu.VMEM((3, 256, 512), BF16),
@@ -179,8 +193,10 @@
             pltpu.VMEM((512, WIDE), BF16),
             pltpu.VMEM((512, 512), F32),
             pltpu.VMEM((512, 512), F32),
-            pltpu.SemaphoreType.DMA((8,)),
-            pltpu.SemaphoreType.DMA((4,)),
+            pltpu.VMEM((1280, 128), F32),
+            pltpu.VMEM((1280, 128), F32),
+            pltpu.SemaphoreType.DMA((9,)),
+            pltpu.SemaphoreType.DMA((5,)),
         ],
         compiler_params=pltpu.CompilerParams(vmem_limit_bytes=50 << 20),
         cost_estimate=pl.CostEstimate(
@@ -198,10 +214,16 @@
     return jnp.broadcast_to(x[row : row + 1, :], (8, 128))
 
 
-NEAR = 4
-
-
-def factor_block(left, right):
+def tree_sum(terms):
+    while len(terms) > 1:
+        terms = [sum(terms[i : i + 2][1:], terms[i]) for i in range(0, len(terms), 2)]
+    return terms[0]
+
+
+NEAR = 5
+
+
+def factor_block(left, right, spread):
     row = lax.broadcasted_iota(jnp.int32, (8, 128), 0)
     left, right = list(left), list(right)
     upper, inverse = [], []
@@ -215,7 +237,12 @@
     for step in range(16):
         near = min(16, step + 1 + NEAR)
         c = [[along_lanes(left[i], 8 * step + l) for l in range(8)] for i in range(step, near)]
-        s = [[along_rows(c[0][l], i) if i >= l else None for l in range(8)] for i in range(8)]
+        for l in range(8):
+            spread[8 * step + l] = c[0][l]
+        s = [
+            [along_rows(spread[8 * step + l, i : i + 1, :], 0) if i >= l else None for l in range(8)]
+            for i in range(8)
+        ]
         lines = [[along_rows(left[step], l) for l in range(8)]]
         lines += [[along_rows(right[step], l) for l in range(8)]]
         lines += c[1:]
@@ -234,9 +261,8 @@
         upper.append(packed(wide_left))
         inverse.append(packed(wide_right))
         for i in range(step + 1, near):
-            for j in range(8):
-                left[i] = left[i] - factors[i - step - 1][j] * wide_left[j]
-                right[i] = right[i] - factors[i - step - 1][j] * wide_right[j]
+            left[i] = left[i] - tree_sum([a * b for a, b in zip(factors[i - step - 1], wide_left)])
+            right[i] = right[i] - tree_sum([a * b for a, b in zip(factors[i - step - 1], wide_right)])
         if near < 16:
             both = jnp.concatenate([upper[-1], inverse[-1]], axis=1)
             change = exact(upper[-1][:, 8 * near :], both, (0, 0))
@@ -249,7 +275,7 @@
 
 def factor_kernel(
     place, mine, other, coeffs, cand_first, cand_second, r_out, new_out,
-    packed, work, c_high, c_low, new, sems, out_sems,
+    packed, work, spread, r_held, c_high, c_low, new, sems, out_sems,
 ):
     copies = []
     for side, cand in enumerate((cand_first, cand_second)):
@@ -275,38 +301,40 @@
                 work[at[a], at[b]] = packed[128 * spot : 128 * spot + 128, :]
                 spot += 1
             else:
-                r_out[at[a], at[b]] = zero
+                r_held[at[a], at[b]] = zero
     for a in range(4):
         first = 128 * a
         upper, inverse = factor_block(
             [work[first + 8 * i : first + 8 * i + 8, at[a]] for i in range(16)],
             [eye[8 * i : 8 * i + 8] for i in range(16)],
+            spread.at[a],
         )
         diag = jnp.where(row >= col, jnp.concatenate(inverse, axis=0), 0.0)
-        r_out[at[a], at[a]] = jnp.where(row <= col, jnp.concatenate(upper, axis=0), 0.0)
+        r_held[at[a], at[a]] = jnp.where(row <= col, jnp.concatenate(upper, axis=0), 0.0)
         work[at[a], beside[a]] = diag
         if a:
             done = slice(512, 512 + first)
             work[at[a], done] = exact(diag, work[at[a], done], (1, 0))
         if a < 3:
             rest = exact(diag, work[at[a], first + 128 : 512], (1, 0))
-            r_out[at[a], first + 128 : 512] = rest
+            r_held[at[a], first + 128 : 512] = rest
             for b in range(a + 1, 4):
                 part = rest[:, 128 * (b - a - 1) : 128 * (b - a)]
                 right = slice(128 * b, 512)
                 work[at[b], right] -= exact(part, rest[:, 128 * (b - a - 1) :], (0, 0))
                 done = slice(512, 512 + first + 128)
                 work[at[b], done] -= exact(part, work[at[a], done], (0, 0))
+    outs = [pltpu.make_async_copy(r_held, r_out, out_sems.at[4])]
+    outs[0].start()
     weight_high, weight_low = halves(exact(coeffs[...], work[:, 512:1024], (0, 0)))
+    weights = jnp.concatenate([weight_high, weight_low], axis=0)
     for copy in copies:
         copy.wait()
-    outs = []
     for chunk in range(4):
         lanes = slice(chunk * 1024, chunk * 1024 + 1024)
-        high, low = c_high[:, lanes], c_low[:, lanes]
-        new[:, lanes] = product(weight_high, high, (1, 0)) + (
-            product(weight_high, low, (1, 0)) + product(weight_low, high, (1, 0))
-        )
+        both = product(weights, c_high[:, lanes], (1, 0))
+        low = product(weight_high, c_low[:, lanes], (1, 0))
+        new[:, lanes] = both[0:128] + (both[128:256] + low)
         outs.append(pltpu.make_async_copy(new.at[:, lanes], new_out.at[:, lanes], out_sems.at[chunk]))
         outs[-1].start()
     for copy in outs:
@@ -321,15 +349,17 @@
             jax.ShapeDtypeStruct((128, 2 * WIDE), F32),
         ),
         in_specs=[SMEM, VMEM, VMEM, VMEM, ANY, ANY],
-        out_specs=(VMEM, ANY),
+        out_specs=(ANY, ANY),
         scratch_shapes=[
             pltpu.VMEM((1280, 128), F32),
             pltpu.VMEM((512, 1024), F32),
+            pltpu.VMEM((4, 128, 8, 128), F32),
+            pltpu.VMEM((512, 512), F32),
             pltpu.VMEM((512, 2 * WIDE), BF16),
             pltpu.VMEM((512, 2 * WIDE), BF16),
             pltpu.VMEM((128, 2 * WIDE), F32),
             pltpu.SemaphoreType.DMA((4,)),
-            pltpu.SemaphoreType.DMA((4,)),
+            pltpu.SemaphoreType.DMA((5,)),
         ],
         compiler_params=pltpu.CompilerParams(vmem_limit_bytes=52 << 20),
         name="factor",
@@ -369,8 +399,8 @@
     return out.reshape(-1, value.shape[-1])
 
 
-def summed(gram):
-    part = scattered_sum(scattered_sum(gram, "core"), "x")
+def summed(keep, send):
+    part = scattered_sum(keep + sent(send, "core", 1), "x")
     part = exchanged_sum(exchanged_sum(part, "y"), "rank")
     mine = gathered(part, "x")
     return mine, sent(mine, "core", 1)
@@ -399,7 +429,8 @@
         inside = lax.dynamic_slice_in_dim(xfactor, jnp.maximum((2 * to - 1) * WIDE, 0), WIDE, 1)
         piece = jnp.where(to == 0, above, inside)
         halos.append(sent(piece, "rank", by) if by else piece)
-    place = jnp.stack([(rank - by) % 4 for by in range(4)]).astype(jnp.int32)
+    core = lax.axis_index("core")
+    place = jnp.stack([(rank - by) % 4 for by in range(4)] + [core]).astype(jnp.int32)
     first = (lax.axis_index(SPACE) * 4 + rank) * sub_elems
     own = lax.dynamic_slice_in_dim(neighbor, rank * sub_elems, sub_elems, 1)
     index_first = tile_index(own[:, :HALO_EL], first - HALO_EL)
@@ -407,12 +438,11 @@
     before, second = transported(
         True, place, index_second, xfactor, mains, None, None, volume, upwind
     )
-    gram, start = transported(
+    keep, send, start = transported(
         False, place, index_first, xfactor, mains, halos, before, volume, upwind
     )
-    mine, other = summed(gram)
-    core = lax.axis_index("core").astype(jnp.int32).reshape(1)
-    r_factor, new_factor = factored(core, mine, other, coeffs, start, second)
+    mine, other = summed(keep, send)
+    r_factor, new_factor = factored(place[4:], mine, other, coeffs, start, second)
     return new_factor, r_factor
 
 

time: 118 us -> 113 us (0.958)
  Pallas kernels: 42.5 us -> 38.8 us
    pallas_call x1, Pallas kernels: 25.3 us -> 21.6 us  [factored(): pl.pallas_call(factor_kernel, out_shape=(jax.ShapeDtypeStruct((512, 512),...]
  transfers between devices with their start and end apart: 21 -> 21, of which waited for: 12 -> 12; matrix products, arithmetic and copies ran while one was open for 3% -> 3% of each run, Pallas kernels for 7% -> 8%
where the time goes in v1:
time: 113 us
  starting transfers between devices  40.2 us (36%)
  Pallas kernels  38.8 us (34%)
  waiting for transfers between devices  27.1 us (24%)
  local copies, waits for them, and re-layouts  4.24 us (4%)
  other arithmetic  1.81 us (2%)
  between operations  1.17 us (1%)
    ppermute x20, starting transfers between devices, sent(): lax.ppermute(value, axis, [(i, (i + by) % count) for i in range(count)])  35.6 us
    ppermute x20, waiting for transfers between devices, sent(): lax.ppermute(value, axis, [(i, (i + by) % count) for i in range(count)])  23.8 us
    pallas_call x1, Pallas kernels, factored(): pl.pallas_call(factor_kernel, out_shape=(jax.ShapeDtypeStruct((512, 512),...  21.6 us
    pallas_call x2, Pallas kernels, transported(): pl.pallas_call(functools.partial(transport_kernel, second), out_shape=(*g...  17.2 us
    ppermute x1, starting transfers between devices, shards(): above = lax.ppermute(above, SPACE, [(i, i + 1) for i in range(count - 1)])  4.59 us
    ppermute x1, waiting for transfers between devices, shards(): above = lax.ppermute(above, SPACE, [(i, i + 1) for i in range(count - 1)])  3.25 us
  transfers between devices with their start and end apart: 21, of which 12 were waited for; matrix products, arithmetic and copies ran while one was open for 3% of the time, Pallas kernels for 8%

profile of v1, /device:TPU:1, one launch (start us, length us, event | category | flops | bytes accessed | tf_op | source)
XLA Modules:
  0.0 113.2 jit_solution(4325438882809717274)
XLA Ops:
  2.2 2.5 %collective-permute-start = (f32[32,4096]{1,0:T(8,128)S(1)}, f32[32,4096]{1,0:T(8,128)S(1)}, u32[]{:S(2)}, u32[]{:S(2)}) collective-permute-start(f32[32,4096]{1,0:T(8,128)S(1)} %get-tuple-element.24), channel_id=1, source_target_pairs={{0,1},{1,2},{2,3},{3,0},{4,5},{5,6},{6,7},{7,4},{8,9},{9,10},{10,1... | collective-permute-start | bytes 1572872 | tf_op jit(solution)/shard_map/ppermute | solution.py:371
  4.7 3.3 %collective-permute-start.1 = (f32[32,4096]{1,0:T(8,128)S(1)}, f32[32,4096]{1,0:T(8,128)S(1)}, u32[]{:S(2)}, u32[]{:S(2)}) collective-permute-start(f32[32,4096]{1,0:T(8,128)S(1)} %get-tuple-element.23), channel_id=1, source_target_pairs={{0,2},{1,3},{2,0},{3,1},{4,6},{5,7},{6,4},{7,5},{8,10},{9,11},{10,... | collective-permute-start | bytes 1572872 | tf_op jit(solution)/shard_map/ppermute | solution.py:371
  8.8 1.7 %slice.10 = f32[32,2048]{1,0:T(8,128)} slice(f32[32,16384]{1,0:T(8,128)} %xfactor.3), slice={[0:32], [14336:16384]} | slice | bytes 524288 | tf_op jit(solution)/shard_map/slice | solution.py:420
  10.4 4.6 %collective-permute-start.3 = (f32[32,2048]{1,0:T(8,128)}, f32[32,2048]{1,0:T(8,128)}, u32[]{:S(2)}, u32[]{:S(2)}) collective-permute-start(f32[32,2048]{1,0:T(8,128)} %slice.10), channel_id=1, source_target_pairs={{0,4},{4,8},{8,12},{12,16},{16,20},{20,24},{24,28},{28,32},{32,36}... | collective-permute-start | bytes 786440 | tf_op jit(solution)/shard_map/ppermute | solution.py:421
  15.4 3.3 %collective-permute-done.3 = f32[32,2048]{1,0:T(8,128)} collective-permute-done((f32[32,2048]{1,0:T(8,128)}, f32[32,2048]{1,0:T(8,128)}, u32[]{:S(2)}, u32[]{:S(2)}) %collective-permute-start.3) | collective-permute-done | bytes 262176 | tf_op jit(solution)/shard_map/ppermute | solution.py:421
  18.6 1.6 %dynamic-slice_select_fusion = (f32[32,2048]{1,0:T(8,128)S(1)}, f32[32,2048]{1,0:T(8,128)S(1)}, f32[32,2048]{1,0:T(8,128)S(1)}, f32[32,2048]{1,0:T(8,128)S(1)}) fusion(f32[32,2048]{1,0:T(8,128)} %collective-permute-done.3, f32[32,16384]{1,0:T(8,128)} %xfactor.3, s32[]{:T(128)S(6)} %max.15, pred[]{:T(512)S(6)} %eq.59, s32[]{:T(128)S(6)} %max.14, pred[]{:T(512)S(6)} %eq.58, ...), kind=kLoop, calls=%fused_computation | loop fusion | flops 262144 | bytes 2359316 | tf_op jit(solution)/shard_map/jit(_where)/select_n | solution.py:430
  21.2 2.3 %collective-permute-start.6 = (f32[32,2048]{1,0:T(8,128)S(1)}, f32[32,2048]{1,0:T(8,128)S(1)}, u32[]{:S(2)}, u32[]{:S(2)}) collective-permute-start(f32[32,2048]{1,0:T(8,128)S(1)} %get-tuple-element.18), channel_id=1, source_target_pairs={{0,3},{1,0},{2,1},{3,2},{4,7},{5,4},{6,5},{7,6},{8,11},{9,8},{10,9... | collective-permute-start | bytes 786440 | tf_op jit(solution)/shard_map/ppermute | solution.py:371
  23.6 7.1 %collective-permute-done.1.refs_1_ = f32[32,4096]{1,0:T(8,128)S(1)} collective-permute-done((f32[32,4096]{1,0:T(8,128)S(1)}, f32[32,4096]{1,0:T(8,128)S(1)}, u32[]{:S(2)}, u32[]{:S(2)}) %collective-permute-start.1) | collective-permute-done | bytes 524320 | tf_op jit(solution)/shard_map/ppermute | solution.py:371
  30.6 8.6 %transport_second.1 = (f32[1280,128]{1,0:T(8,128)S(1)}, bf16[2,512,2048]{2,1,0:T(8,128)(2,1)}) custom-call(s32[5]{0:T(128)S(1)} %stack.23.place, s32[3,32]{1,0:T(4,128)S(1)} %get-tuple-element.28.index, f32[32,16384]{1,0:T(8,128)} %xfactor.3, f32[32,4096]{1,0:T(8,128)S(1)} %collective-permute-done.refs_0_, f32[32,4096]{1,0:T(8,128)S(1)} %collective-permute-done.1.refs_1_, ...), custom_call_target="tpu_custom_call" | custom-call | flops 8999999488 | bytes 8388608 | tf_op jit(solution)/shard_map/transport_second/pallas_call | solution.py:181
  40.1 1.7 %collective-permute-done.5.refs_5_ = f32[32,2048]{1,0:T(8,128)S(1)} collective-permute-done((f32[32,2048]{1,0:T(8,128)S(1)}, f32[32,2048]{1,0:T(8,128)S(1)}, u32[]{:S(2)}, u32[]{:S(2)}) %collective-permute-start.5) | collective-permute-done | bytes 262176 | tf_op jit(solution)/shard_map/ppermute | solution.py:371
  41.9 8.5 %transport_first.1 = (f32[640,128]{1,0:T(8,128)S(1)}, f32[640,128]{1,0:T(8,128)S(1)}, bf16[2,512,2048]{2,1,0:T(8,128)(2,1)}) custom-call(s32[5]{0:T(128)S(1)} %stack.23.place, s32[3,32]{1,0:T(4,128)S(1)} %get-tuple-element.29.index, f32[32,16384]{1,0:T(8,128)} %xfactor.3, f32[32,4096]{1,0:T(8,128)S(1)} %collective-permute-done.refs_0_, ...), custom_call_target="tpu_custom_call" | custom-call | flops 8999999488 | bytes 8388608 | tf_op jit(solution)/shard_map/transport_first/pallas_call | solution.py:181
  53.4 2.6 %collective-permute-start.10 = (f32[160,128]{1,0:T(8,128)S(1)}, f32[160,128]{1,0:T(8,128)S(1)}, u32[]{:S(2)}, u32[]{:S(2)}) collective-permute-start(f32[160,128]{1,0:T(8,128)S(1)} %get-tuple-element.26), channel_id=1, source_target_pairs={{0,96},{32,0},{64,32},{96,64},{1,97},{33,1},{65,33},{97,65},{2,98}... | collective-permute-start | bytes 245768 | tf_op jit(solution)/shard_map/ppermute | solution.py:371
  55.9 1.7 %collective-permute-start.9 = (f32[160,128]{1,0:T(8,128)S(1)}, f32[160,128]{1,0:T(8,128)S(1)}, u32[]{:S(2)}, u32[]{:S(2)}) collective-permute-start(f32[160,128]{1,0:T(8,128)S(1)} %get-tuple-element.27), channel_id=1, source_target_pairs={{0,64},{32,96},{64,0},{96,32},{1,65},{33,97},{65,1},{97,33},{2,66}... | collective-permute-start | bytes 245768 | tf_op jit(solution)/shard_map/ppermute | solution.py:371
  57.7 4.0 %collective-permute-done.8 = f32[160,128]{1,0:T(8,128)S(1)} collective-permute-done((f32[160,128]{1,0:T(8,128)S(1)}, f32[160,128]{1,0:T(8,128)S(1)}, u32[]{:S(2)}, u32[]{:S(2)}) %collective-permute-start.8) | collective-permute-done | bytes 81952 | tf_op jit(solution)/shard_map/ppermute | solution.py:371
  61.9 3.0 %collective-permute-start.11 = (f32[160,128]{1,0:T(8,128)S(1)}, f32[160,128]{1,0:T(8,128)S(1)}, u32[]{:S(2)}, u32[]{:S(2)}) collective-permute-start(f32[160,128]{1,0:T(8,128)S(1)} %fusion.1), channel_id=1, source_target_pairs={{0,16},{8,24},{16,0},{24,8},{1,17},{9,25},{17,1},{25,9},{2,18},{10... | collective-permute-start | bytes 245768 | tf_op jit(solution)/shard_map/ppermute | solution.py:371
  65.3 2.3 %collective-permute-start.13 = (f32[160,128]{1,0:T(8,128)S(1)}, f32[160,128]{1,0:T(8,128)S(1)}, u32[]{:S(2)}, u32[]{:S(2)}) collective-permute-start(f32[160,128]{1,0:T(8,128)S(1)} %fusion.1), channel_id=1, source_target_pairs={{0,24},{8,0},{16,8},{24,16},{1,25},{9,1},{17,9},{25,17},{2,26},{10... | collective-permute-start | bytes 245768 | tf_op jit(solution)/shard_map/ppermute | solution.py:371
  67.6 2.5 %collective-permute-done.12 = f32[160,128]{1,0:T(8,128)S(1)} collective-permute-done((f32[160,128]{1,0:T(8,128)S(1)}, f32[160,128]{1,0:T(8,128)S(1)}, u32[]{:S(2)}, u32[]{:S(2)}) %collective-permute-start.12) | collective-permute-done | bytes 81952 | tf_op jit(solution)/shard_map/ppermute | solution.py:371
  70.1 2.0 %collective-permute-start.14 = (f32[160,128]{1,0:T(8,128)S(1)}, f32[160,128]{1,0:T(8,128)S(1)}, u32[]{:S(2)}, u32[]{:S(2)}) collective-permute-start(f32[160,128]{1,0:T(8,128)S(1)} %add_add_fusion.1), channel_id=1, source_target_pairs={{0,2},{1,3},{2,0},{3,1},{4,6},{5,7},{6,4},{7,5},{8,10},{9,11},{10,... | collective-permute-start | bytes 245768 | tf_op jit(solution)/shard_map/ppermute | solution.py:371
  72.2 2.0 %collective-permute-start.15 = (f32[160,128]{1,0:T(8,128)S(1)}, f32[160,128]{1,0:T(8,128)S(1)}, u32[]{:S(2)}, u32[]{:S(2)}) collective-permute-start(f32[160,128]{1,0:T(8,128)S(1)} %add_add_fusion.1), channel_id=1, source_target_pairs={{0,1},{1,2},{2,3},{3,0},{4,5},{5,6},{6,7},{7,4},{8,9},{9,10},{10,1... | collective-permute-start | bytes 245768 | tf_op jit(solution)/shard_map/ppermute | solution.py:371
  74.2 2.3 %collective-permute-start.16 = (f32[160,128]{1,0:T(8,128)S(1)}, f32[160,128]{1,0:T(8,128)S(1)}, u32[]{:S(2)}, u32[]{:S(2)}) collective-permute-start(f32[160,128]{1,0:T(8,128)S(1)} %add_add_fusion.1), channel_id=1, source_target_pairs={{0,3},{1,0},{2,1},{3,2},{4,7},{5,4},{6,5},{7,6},{8,11},{9,8},{10,9... | collective-permute-start | bytes 245768 | tf_op jit(solution)/shard_map/ppermute | solution.py:371
  76.5 2.5 %collective-permute-done.15 = f32[160,128]{1,0:T(8,128)S(1)} collective-permute-done((f32[160,128]{1,0:T(8,128)S(1)}, f32[160,128]{1,0:T(8,128)S(1)}, u32[]{:S(2)}, u32[]{:S(2)}) %collective-permute-start.15) | collective-permute-done | bytes 81952 | tf_op jit(solution)/shard_map/ppermute | solution.py:371
  79.2 2.8 %collective-permute-start.18 = (f32[160,128]{1,0:T(8,128)S(1)}, f32[160,128]{1,0:T(8,128)S(1)}, u32[]{:S(2)}, u32[]{:S(2)}) collective-permute-start(f32[160,128]{1,0:T(8,128)S(1)} %get-tuple-element.17), channel_id=1, source_target_pairs={{0,64},{32,96},{64,0},{96,32},{1,65},{33,97},{65,1},{97,33},{2,66}... | collective-permute-start | bytes 245768 | tf_op jit(solution)/shard_map/ppermute | solution.py:371
  85.3 4.9 %collective-permute-start.20 = (f32[640,128]{1,0:T(8,128)S(1)}, f32[640,128]{1,0:T(8,128)S(1)}, u32[]{:S(2)}, u32[]{:S(2)}) collective-permute-start(f32[640,128]{1,0:T(8,128)S(1)} %bitcast.27), channel_id=1, source_target_pairs={{0,4},{4,0},{1,5},{5,1},{2,6},{6,2},{3,7},{7,3},{8,12},{12,8},{9,1... | collective-permute-start | bytes 983048 | tf_op jit(solution)/shard_map/ppermute | solution.py:371
  91.5 21.6 %factor.1 = (f32[512,512]{1,0:T(8,128)}, f32[128,4096]{1,0:T(8,128)}) custom-call(s32[1]{0:T(128)} %bitcast.place, f32[640,128]{1,0:T(8,128)S(1)} %bitcast.28, f32[640,128]{1,0:T(8,128)S(1)} %collective-permute-done.20.other, f32[512,128]{1,0:T(8,128)S(1)} %copy-done.1, bf16[2,512,2048]{2,1,0:T(8,128)(2,1)} %get-tuple-element.12.cand_first, ...), custom_call_target="tpu_custom_call" | custom-call | tf_op jit(solution)/shard_map/factor/pallas_call | solution.py:345
  (47 shorter events, 12.6 us)
Async XLA Ops:
  2.2 28.5 %copy-start.2 = (f32[3,64,64]{2,1,0:T(8,128)S(1)}, f32[3,64,64]{2,1,0:T(8,128)}, u32[]{:S(2)}) copy-start(f32[3,64,64]{2,1,0:T(8,128)} %refs_8_.1) | copy-start | bytes 147460
  2.2 28.5 %copy-start.3 = (f32[3,64,64]{2,1,0:T(8,128)S(1)}, f32[3,64,64]{2,1,0:T(8,128)}, u32[]{:S(2)}) copy-start(f32[3,64,64]{2,1,0:T(8,128)} %refs_9_.1) | copy-start | bytes 147460
  2.2 19.1 %collective-permute-start = (f32[32,4096]{1,0:T(8,128)S(1)}, f32[32,4096]{1,0:T(8,128)S(1)}, u32[]{:S(2)}, u32[]{:S(2)}) collective-permute-start(f32[32,4096]{1,0:T(8,128)S(1)} %get-tuple-element.24), channel_id=1, source_target_pairs={{0,1},{1,2},{2,3},{3,0},{4,5},{5,6},{6,7},{7,4},{8,9},{9,10},{10,1... | collective-permute-start | bytes 1572872 | tf_op jit(solution)/shard_map/ppermute | solution.py:371
  4.7 25.9 %collective-permute-start.1 = (f32[32,4096]{1,0:T(8,128)S(1)}, f32[32,4096]{1,0:T(8,128)S(1)}, u32[]{:S(2)}, u32[]{:S(2)}) collective-permute-start(f32[32,4096]{1,0:T(8,128)S(1)} %get-tuple-element.23), channel_id=1, source_target_pairs={{0,2},{1,3},{2,0},{3,1},{4,6},{5,7},{6,4},{7,5},{8,10},{9,11},{10,... | collective-permute-start | bytes 1572872 | tf_op jit(solution)/shard_map/ppermute | solution.py:371
  8.0 22.6 %collective-permute-start.2 = (f32[32,4096]{1,0:T(8,128)S(1)}, f32[32,4096]{1,0:T(8,128)S(1)}, u32[]{:S(2)}, u32[]{:S(2)}) collective-permute-start(f32[32,4096]{1,0:T(8,128)S(1)} %get-tuple-element.22), channel_id=1, source_target_pairs={{0,3},{1,0},{2,1},{3,2},{4,7},{5,4},{6,5},{7,6},{8,11},{9,8},{10,9... | collective-permute-start | bytes 1572872 | tf_op jit(solution)/shard_map/ppermute | solution.py:371
  10.4 8.2 %collective-permute-start.3 = (f32[32,2048]{1,0:T(8,128)}, f32[32,2048]{1,0:T(8,128)}, u32[]{:S(2)}, u32[]{:S(2)}) collective-permute-start(f32[32,2048]{1,0:T(8,128)} %slice.10), channel_id=1, source_target_pairs={{0,4},{4,8},{8,12},{12,16},{16,20},{20,24},{24,28},{28,32},{32,36}... | collective-permute-start | bytes 786440 | tf_op jit(solution)/shard_map/ppermute | solution.py:421
  20.3 19.9 %collective-permute-start.4 = (f32[32,2048]{1,0:T(8,128)S(1)}, f32[32,2048]{1,0:T(8,128)S(1)}, u32[]{:S(2)}, u32[]{:S(2)}) collective-permute-start(f32[32,2048]{1,0:T(8,128)S(1)} %get-tuple-element.20), channel_id=1, source_target_pairs={{0,1},{1,2},{2,3},{3,0},{4,5},{5,6},{6,7},{7,4},{8,9},{9,10},{10,1... | collective-permute-start | bytes 786440 | tf_op jit(solution)/shard_map/ppermute | solution.py:371
  21.1 20.8 %collective-permute-start.5 = (f32[32,2048]{1,0:T(8,128)S(1)}, f32[32,2048]{1,0:T(8,128)S(1)}, u32[]{:S(2)}, u32[]{:S(2)}) collective-permute-start(f32[32,2048]{1,0:T(8,128)S(1)} %get-tuple-element.19), channel_id=1, source_target_pairs={{0,2},{1,3},{2,0},{3,1},{4,6},{5,7},{6,4},{7,5},{8,10},{9,11},{10,... | collective-permute-start | bytes 786440 | tf_op jit(solution)/shard_map/ppermute | solution.py:371
  21.2 20.6 %collective-permute-start.6 = (f32[32,2048]{1,0:T(8,128)S(1)}, f32[32,2048]{1,0:T(8,128)S(1)}, u32[]{:S(2)}, u32[]{:S(2)}) collective-permute-start(f32[32,2048]{1,0:T(8,128)S(1)} %get-tuple-element.18), channel_id=1, source_target_pairs={{0,3},{1,0},{2,1},{3,2},{4,7},{5,4},{6,5},{7,6},{8,11},{9,8},{10,9... | collective-permute-start | bytes 786440 | tf_op jit(solution)/shard_map/ppermute | solution.py:371
  50.4 41.0 %copy-start.1 = (f32[512,128]{1,0:T(8,128)S(1)}, f32[512,128]{1,0:T(8,128)}, u32[]{:S(2)}) copy-start(f32[512,128]{1,0:T(8,128)} %coeffs.1) | copy-start | bytes 786436
  50.4 2.9 %collective-permute-start.7 = (f32[640,128]{1,0:T(8,128)S(1)}, f32[640,128]{1,0:T(8,128)S(1)}, u32[]{:S(2)}, u32[]{:S(2)}) collective-permute-start(f32[640,128]{1,0:T(8,128)S(1)} %get-tuple-element.11), channel_id=1, source_target_pairs={{0,4},{4,0},{1,5},{5,1},{2,6},{6,2},{3,7},{7,3},{8,12},{12,8},{9,1... | collective-permute-start | bytes 983048 | tf_op jit(solution)/shard_map/ppermute | solution.py:371
  53.4 4.3 %collective-permute-start.10 = (f32[160,128]{1,0:T(8,128)S(1)}, f32[160,128]{1,0:T(8,128)S(1)}, u32[]{:S(2)}, u32[]{:S(2)}) collective-permute-start(f32[160,128]{1,0:T(8,128)S(1)} %get-tuple-element.26), channel_id=1, source_target_pairs={{0,96},{32,0},{64,32},{96,64},{1,97},{33,1},{65,33},{97,65},{2,98}... | collective-permute-start | bytes 245768 | tf_op jit(solution)/shard_map/ppermute | solution.py:371
  55.9 5.7 %collective-permute-start.8 = (f32[160,128]{1,0:T(8,128)S(1)}, f32[160,128]{1,0:T(8,128)S(1)}, u32[]{:S(2)}, u32[]{:S(2)}) collective-permute-start(f32[160,128]{1,0:T(8,128)S(1)} %get-tuple-element.25), channel_id=1, source_target_pairs={{0,32},{32,64},{64,96},{96,0},{1,33},{33,65},{65,97},{97,1},{2,34}... | collective-permute-start | bytes 245768 | tf_op jit(solution)/shard_map/ppermute | solution.py:371
  55.9 6.0 %collective-permute-start.9 = (f32[160,128]{1,0:T(8,128)S(1)}, f32[160,128]{1,0:T(8,128)S(1)}, u32[]{:S(2)}, u32[]{:S(2)}) collective-permute-start(f32[160,128]{1,0:T(8,128)S(1)} %get-tuple-element.27), channel_id=1, source_target_pairs={{0,64},{32,96},{64,0},{96,32},{1,65},{33,97},{65,1},{97,33},{2,66}... | collective-permute-start | bytes 245768 | tf_op jit(solution)/shard_map/ppermute | solution.py:371
  61.9 5.7 %collective-permute-start.11 = (f32[160,128]{1,0:T(8,128)S(1)}, f32[160,128]{1,0:T(8,128)S(1)}, u32[]{:S(2)}, u32[]{:S(2)}) collective-permute-start(f32[160,128]{1,0:T(8,128)S(1)} %fusion.1), channel_id=1, source_target_pairs={{0,16},{8,24},{16,0},{24,8},{1,17},{9,25},{17,1},{25,9},{2,18},{10... | collective-permute-start | bytes 245768 | tf_op jit(solution)/shard_map/ppermute | solution.py:371
  64.9 5.2 %collective-permute-start.12 = (f32[160,128]{1,0:T(8,128)S(1)}, f32[160,128]{1,0:T(8,128)S(1)}, u32[]{:S(2)}, u32[]{:S(2)}) collective-permute-start(f32[160,128]{1,0:T(8,128)S(1)} %fusion.1), channel_id=1, source_target_pairs={{0,8},{8,16},{16,24},{24,0},{1,9},{9,17},{17,25},{25,1},{2,10},{10... | collective-permute-start | bytes 245768 | tf_op jit(solution)/shard_map/ppermute | solution.py:371
  65.3 4.8 %collective-permute-start.13 = (f32[160,128]{1,0:T(8,128)S(1)}, f32[160,128]{1,0:T(8,128)S(1)}, u32[]{:S(2)}, u32[]{:S(2)}) collective-permute-start(f32[160,128]{1,0:T(8,128)S(1)} %fusion.1), channel_id=1, source_target_pairs={{0,24},{8,0},{16,8},{24,16},{1,25},{9,1},{17,9},{25,17},{2,26},{10... | collective-permute-start | bytes 245768 | tf_op jit(solution)/shard_map/ppermute | solution.py:371
  70.1 6.3 %collective-permute-start.14 = (f32[160,128]{1,0:T(8,128)S(1)}, f32[160,128]{1,0:T(8,128)S(1)}, u32[]{:S(2)}, u32[]{:S(2)}) collective-permute-start(f32[160,128]{1,0:T(8,128)S(1)} %add_add_fusion.1), channel_id=1, source_target_pairs={{0,2},{1,3},{2,0},{3,1},{4,6},{5,7},{6,4},{7,5},{8,10},{9,11},{10,... | collective-permute-start | bytes 245768 | tf_op jit(solution)/shard_map/ppermute | solution.py:371
  72.2 6.8 %collective-permute-start.15 = (f32[160,128]{1,0:T(8,128)S(1)}, f32[160,128]{1,0:T(8,128)S(1)}, u32[]{:S(2)}, u32[]{:S(2)}) collective-permute-start(f32[160,128]{1,0:T(8,128)S(1)} %add_add_fusion.1), channel_id=1, source_target_pairs={{0,1},{1,2},{2,3},{3,0},{4,5},{5,6},{6,7},{7,4},{8,9},{9,10},{10,1... | collective-permute-start | bytes 245768 | tf_op jit(solution)/shard_map/ppermute | solution.py:371
  74.2 4.8 %collective-permute-start.16 = (f32[160,128]{1,0:T(8,128)S(1)}, f32[160,128]{1,0:T(8,128)S(1)}, u32[]{:S(2)}, u32[]{:S(2)}) collective-permute-start(f32[160,128]{1,0:T(8,128)S(1)} %add_add_fusion.1), channel_id=1, source_target_pairs={{0,3},{1,0},{2,1},{3,2},{4,7},{5,4},{6,5},{7,6},{8,11},{9,8},{10,9... | collective-permute-start | bytes 245768 | tf_op jit(solution)/shard_map/ppermute | solution.py:371
  79.0 4.6 %collective-permute-start.17 = (f32[160,128]{1,0:T(8,128)S(1)}, f32[160,128]{1,0:T(8,128)S(1)}, u32[]{:S(2)}, u32[]{:S(2)}) collective-permute-start(f32[160,128]{1,0:T(8,128)S(1)} %get-tuple-element.17), channel_id=1, source_target_pairs={{0,32},{32,64},{64,96},{96,0},{1,33},{33,65},{65,97},{97,1},{2,34}... | collective-permute-start | bytes 245768 | tf_op jit(solution)/shard_map/ppermute | solution.py:371
  79.2 5.5 %collective-permute-start.18 = (f32[160,128]{1,0:T(8,128)S(1)}, f32[160,128]{1,0:T(8,128)S(1)}, u32[]{:S(2)}, u32[]{:S(2)}) collective-permute-start(f32[160,128]{1,0:T(8,128)S(1)} %get-tuple-element.17), channel_id=1, source_target_pairs={{0,64},{32,96},{64,0},{96,32},{1,65},{33,97},{65,1},{97,33},{2,66}... | collective-permute-start | bytes 245768 | tf_op jit(solution)/shard_map/ppermute | solution.py:371
  82.0 3.3 %collective-permute-start.19 = (f32[160,128]{1,0:T(8,128)S(1)}, f32[160,128]{1,0:T(8,128)S(1)}, u32[]{:S(2)}, u32[]{:S(2)}) collective-permute-start(f32[160,128]{1,0:T(8,128)S(1)} %get-tuple-element.17), channel_id=1, source_target_pairs={{0,96},{32,0},{64,32},{96,64},{1,97},{33,1},{65,33},{97,65},{2,98}... | collective-permute-start | bytes 245768 | tf_op jit(solution)/shard_map/ppermute | solution.py:371
  85.3 6.2 %collective-permute-start.20 = (f32[640,128]{1,0:T(8,128)S(1)}, f32[640,128]{1,0:T(8,128)S(1)}, u32[]{:S(2)}, u32[]{:S(2)}) collective-permute-start(f32[640,128]{1,0:T(8,128)S(1)} %bitcast.27), channel_id=1, source_target_pairs={{0,4},{4,0},{1,5},{5,1},{2,6},{6,2},{3,7},{7,3},{8,12},{12,8},{9,1... | collective-permute-start | bytes 983048 | tf_op jit(solution)/shard_map/ppermute | solution.py:371
  (2 other events, 15.2 us)

commit v2 on v1

--- a/solution.py
+++ b/solution.py
@@ -61,7 +61,7 @@
             to = window.at[piece, :, side * WIDE : side * WIDE + WIDE]
             copies.append(pltpu.make_async_copy(sources[side], to, in_sems.at[2 * piece + side]))
     if not second:
-        copies.append(pltpu.make_async_copy(before, added, in_sems.at[8]))
+        copies.append(pltpu.make_async_copy(before.at[0:1280, :], added, in_sems.at[8]))
     for copy in copies:
         copy.start()
 
@@ -163,7 +163,7 @@
             packed[to, :] = total if second else total + added[to, :]
             spot += 1
     if second:
-        outs.append(pltpu.make_async_copy(packed, grams[0], out_sems.at[4]))
+        outs.append(pltpu.make_async_copy(packed, grams[0].at[0:1280, :], out_sems.at[4]))
         outs[-1].start()
     else:
         for half in range(2):
@@ -419,18 +419,19 @@
     count = lax.axis_size(SPACE)
     above = xfactor[:, 7 * WIDE :]
     above = lax.ppermute(above, SPACE, [(i, i + 1) for i in range(count - 1)])
+    order = (2, 1, 3)
     mains, halos = [], []
-    for by in range(1, 4):
+    for by in order:
         to = (rank + by) % 4
         piece = lax.dynamic_slice_in_dim(xfactor, to * 2 * WIDE, 2 * WIDE, 1)
         mains.append(sent(piece, "rank", by))
-    for by in range(4):
+    for by in (0, *order):
         to = (rank + by) % 4
         inside = lax.dynamic_slice_in_dim(xfactor, jnp.maximum((2 * to - 1) * WIDE, 0), WIDE, 1)
         piece = jnp.where(to == 0, above, inside)
         halos.append(sent(piece, "rank", by) if by else piece)
     core = lax.axis_index("core")
-    place = jnp.stack([(rank - by) % 4 for by in range(4)] + [core]).astype(jnp.int32)
+    place = jnp.stack([(rank - by) % 4 for by in (0, *order)] + [core]).astype(jnp.int32)
     first = (lax.axis_index(SPACE) * 4 + rank) * sub_elems
     own = lax.dynamic_slice_in_dim(neighbor, rank * sub_elems, sub_elems, 1)
     index_first = tile_index(own[:, :HALO_EL], first - HALO_EL)

time: 113 us -> 112 us (level)
    ppermute x20, waiting for transfers between devices: 23.8 us -> 22.7 us  [sent(): lax.ppermute(value, axis, [(i, (i + by) % count) for i in range(count)])]
  transfers between devices with their start and end apart: 21 -> 21, of which waited for: 12 -> 13; matrix products, arithmetic and copies ran while one was open for 3% -> 3% of each run, Pallas kernels for 8% -> 8%
where the time goes in v2:
time: 112 us; the launch traced here: 111 us
  starting transfers between devices  39.4 us (35%)
  Pallas kernels  38.7 us (35%)
  waiting for transfers between devices  26 us (23%)
  local copies, waits for them, and re-layouts  4.24 us (4%)
  other arithmetic  1.81 us (2%)
  between operations  1.18 us (1%)
    ppermute x20, starting transfers between devices, sent(): lax.ppermute(value, axis, [(i, (i + by) % count) for i in range(count)])  34.8 us
    ppermute x20, waiting for transfers between devices, sent(): lax.ppermute(value, axis, [(i, (i + by) % count) for i in range(count)])  22.7 us
    pallas_call x1, Pallas kernels, factored(): pl.pallas_call(factor_kernel, out_shape=(jax.ShapeDtypeStruct((512, 512),...  21.6 us
    pallas_call x2, Pallas kernels, transported(): pl.pallas_call(functools.partial(transport_kernel, second), out_shape=(*g...  17.2 us
    ppermute x1, starting transfers between devices, shards(): above = lax.ppermute(above, SPACE, [(i, i + 1) for i in range(count - 1)])  4.59 us
    ppermute x1, waiting for transfers between devices, shards(): above = lax.ppermute(above, SPACE, [(i, i + 1) for i in range(count - 1)])  3.25 us
  transfers between devices with their start and end apart: 21, of which 13 were waited for; matrix products, arithmetic and copies ran while one was open for 3% of the time, Pallas kernels for 8%

profile of v2, /device:TPU:1, one launch (start us, length us, event | category | flops | bytes accessed | tf_op | source)
XLA Modules:
  0.0 111.3 jit_solution(5569123160385919213)
XLA Ops:
  0.7 1.5 %constant_dynamic-slice_fusion = (f32[32,4096]{1,0:T(8,128)S(1)}, f32[32,4096]{1,0:T(8,128)S(1)}, f32[32,4096]{1,0:T(8,128)S(1)}) fusion(f32[32,16384]{1,0:T(8,128)} %xfactor.3, s32[]{:T(128)S(6)} %select_n.202, s32[]{:T(128)S(6)} %select_n.200, s32[]{:T(128)S(6)} %select_n.198), kind=kLoop, calls=%fused_computation.16 | loop fusion | bytes 3145740 | tf_op jit(solution)/shard_map/dynamic_slice | solution.py:426
  2.2 4.5 %collective-permute-start = (f32[32,4096]{1,0:T(8,128)S(1)}, f32[32,4096]{1,0:T(8,128)S(1)}, u32[]{:S(2)}, u32[]{:S(2)}) collective-permute-start(f32[32,4096]{1,0:T(8,128)S(1)} %get-tuple-element.24), channel_id=1, source_target_pairs={{0,2},{1,3},{2,0},{3,1},{4,6},{5,7},{6,4},{7,5},{8,10},{9,11},{10,... | collective-permute-start | bytes 1572872 | tf_op jit(solution)/shard_map/ppermute | solution.py:371
  7.4 1.9 %collective-permute-start.2 = (f32[32,4096]{1,0:T(8,128)S(1)}, f32[32,4096]{1,0:T(8,128)S(1)}, u32[]{:S(2)}, u32[]{:S(2)}) collective-permute-start(f32[32,4096]{1,0:T(8,128)S(1)} %get-tuple-element.22), channel_id=1, source_target_pairs={{0,3},{1,0},{2,1},{3,2},{4,7},{5,4},{6,5},{7,6},{8,11},{9,8},{10,9... | collective-permute-start | bytes 1572872 | tf_op jit(solution)/shard_map/ppermute | solution.py:371
  9.4 1.7 %slice.10 = f32[32,2048]{1,0:T(8,128)} slice(f32[32,16384]{1,0:T(8,128)} %xfactor.3), slice={[0:32], [14336:16384]} | slice | bytes 524288 | tf_op jit(solution)/shard_map/slice | solution.py:420
  11.0 4.6 %collective-permute-start.3 = (f32[32,2048]{1,0:T(8,128)}, f32[32,2048]{1,0:T(8,128)}, u32[]{:S(2)}, u32[]{:S(2)}) collective-permute-start(f32[32,2048]{1,0:T(8,128)} %slice.10), channel_id=1, source_target_pairs={{0,4},{4,8},{8,12},{12,16},{16,20},{20,24},{24,28},{28,32},{32,36}... | collective-permute-start | bytes 786440 | tf_op jit(solution)/shard_map/ppermute | solution.py:421
  16.0 3.3 %collective-permute-done.3 = f32[32,2048]{1,0:T(8,128)} collective-permute-done((f32[32,2048]{1,0:T(8,128)}, f32[32,2048]{1,0:T(8,128)}, u32[]{:S(2)}, u32[]{:S(2)}) %collective-permute-start.3) | collective-permute-done | bytes 262176 | tf_op jit(solution)/shard_map/ppermute | solution.py:421
  19.3 1.6 %dynamic-slice_select_fusion = (f32[32,2048]{1,0:T(8,128)S(1)}, f32[32,2048]{1,0:T(8,128)S(1)}, f32[32,2048]{1,0:T(8,128)S(1)}, f32[32,2048]{1,0:T(8,128)S(1)}) fusion(f32[32,2048]{1,0:T(8,128)} %collective-permute-done.3, f32[32,16384]{1,0:T(8,128)} %xfactor.3, s32[]{:T(128)S(6)} %max.15, pred[]{:T(512)S(6)} %eq.59, s32[]{:T(128)S(6)} %max.14, pred[]{:T(512)S(6)} %eq.58, ...), kind=kLoop, calls=%fused_computation | loop fusion | flops 262144 | bytes 2359316 | tf_op jit(solution)/shard_map/jit(_where)/select_n | solution.py:431
  21.3 2.5 %collective-permute-start.6 = (f32[32,2048]{1,0:T(8,128)S(1)}, f32[32,2048]{1,0:T(8,128)S(1)}, u32[]{:S(2)}, u32[]{:S(2)}) collective-permute-start(f32[32,2048]{1,0:T(8,128)S(1)} %get-tuple-element.18), channel_id=1, source_target_pairs={{0,3},{1,0},{2,1},{3,2},{4,7},{5,4},{6,5},{7,6},{8,11},{9,8},{10,9... | collective-permute-start | bytes 786440 | tf_op jit(solution)/shard_map/ppermute | solution.py:371
  23.7 7.3 %collective-permute-done.1.refs_1_ = f32[32,4096]{1,0:T(8,128)S(1)} collective-permute-done((f32[32,4096]{1,0:T(8,128)S(1)}, f32[32,4096]{1,0:T(8,128)S(1)}, u32[]{:S(2)}, u32[]{:S(2)}) %collective-permute-start.1) | collective-permute-done | bytes 524320 | tf_op jit(solution)/shard_map/ppermute | solution.py:371
  31.0 8.6 %transport_second.1 = (f32[1280,128]{1,0:T(8,128)S(1)}, bf16[2,512,2048]{2,1,0:T(8,128)(2,1)}) custom-call(s32[5]{0:T(128)S(1)} %stack.23.place, s32[3,32]{1,0:T(4,128)S(1)} %get-tuple-element.28.index, f32[32,16384]{1,0:T(8,128)} %xfactor.3, f32[32,4096]{1,0:T(8,128)S(1)} %collective-permute-done.refs_0_, f32[32,4096]{1,0:T(8,128)S(1)} %collective-permute-done.1.refs_1_, ...), custom_call_target="tpu_custom_call" | custom-call | flops 8999999488 | bytes 8388608 | tf_op jit(solution)/shard_map/transport_second/pallas_call | solution.py:181
  41.6 8.5 %transport_first.1 = (f32[640,128]{1,0:T(8,128)S(1)}, f32[640,128]{1,0:T(8,128)S(1)}, bf16[2,512,2048]{2,1,0:T(8,128)(2,1)}) custom-call(s32[5]{0:T(128)S(1)} %stack.23.place, s32[3,32]{1,0:T(4,128)S(1)} %get-tuple-element.29.index, f32[32,16384]{1,0:T(8,128)} %xfactor.3, f32[32,4096]{1,0:T(8,128)S(1)} %collective-permute-done.refs_0_, ...), custom_call_target="tpu_custom_call" | custom-call | flops 8999999488 | bytes 8388608 | tf_op jit(solution)/shard_map/transport_first/pallas_call | solution.py:181
  52.8 2.5 %collective-permute-start.10 = (f32[160,128]{1,0:T(8,128)S(1)}, f32[160,128]{1,0:T(8,128)S(1)}, u32[]{:S(2)}, u32[]{:S(2)}) collective-permute-start(f32[160,128]{1,0:T(8,128)S(1)} %get-tuple-element.26), channel_id=1, source_target_pairs={{0,96},{32,0},{64,32},{96,64},{1,97},{33,1},{65,33},{97,65},{2,98}... | collective-permute-start | bytes 245768 | tf_op jit(solution)/shard_map/ppermute | solution.py:371
  55.4 1.7 %collective-permute-start.9 = (f32[160,128]{1,0:T(8,128)S(1)}, f32[160,128]{1,0:T(8,128)S(1)}, u32[]{:S(2)}, u32[]{:S(2)}) collective-permute-start(f32[160,128]{1,0:T(8,128)S(1)} %get-tuple-element.27), channel_id=1, source_target_pairs={{0,64},{32,96},{64,0},{96,32},{1,65},{33,97},{65,1},{97,33},{2,66}... | collective-permute-start | bytes 245768 | tf_op jit(solution)/shard_map/ppermute | solution.py:371
  57.1 4.0 %collective-permute-done.8 = f32[160,128]{1,0:T(8,128)S(1)} collective-permute-done((f32[160,128]{1,0:T(8,128)S(1)}, f32[160,128]{1,0:T(8,128)S(1)}, u32[]{:S(2)}, u32[]{:S(2)}) %collective-permute-start.8) | collective-permute-done | bytes 81952 | tf_op jit(solution)/shard_map/ppermute | solution.py:371
  61.4 3.0 %collective-permute-start.11 = (f32[160,128]{1,0:T(8,128)S(1)}, f32[160,128]{1,0:T(8,128)S(1)}, u32[]{:S(2)}, u32[]{:S(2)}) collective-permute-start(f32[160,128]{1,0:T(8,128)S(1)} %fusion.1), channel_id=1, source_target_pairs={{0,16},{8,24},{16,0},{24,8},{1,17},{9,25},{17,1},{25,9},{2,18},{10... | collective-permute-start | bytes 245768 | tf_op jit(solution)/shard_map/ppermute | solution.py:371
  64.8 2.3 %collective-permute-start.13 = (f32[160,128]{1,0:T(8,128)S(1)}, f32[160,128]{1,0:T(8,128)S(1)}, u32[]{:S(2)}, u32[]{:S(2)}) collective-permute-start(f32[160,128]{1,0:T(8,128)S(1)} %fusion.1), channel_id=1, source_target_pairs={{0,24},{8,0},{16,8},{24,16},{1,25},{9,1},{17,9},{25,17},{2,26},{10... | collective-permute-start | bytes 245768 | tf_op jit(solution)/shard_map/ppermute | solution.py:371
  67.1 2.5 %collective-permute-done.12 = f32[160,128]{1,0:T(8,128)S(1)} collective-permute-done((f32[160,128]{1,0:T(8,128)S(1)}, f32[160,128]{1,0:T(8,128)S(1)}, u32[]{:S(2)}, u32[]{:S(2)}) %collective-permute-start.12) | collective-permute-done | bytes 81952 | tf_op jit(solution)/shard_map/ppermute | solution.py:371
  69.6 1.8 %collective-permute-start.14 = (f32[160,128]{1,0:T(8,128)S(1)}, f32[160,128]{1,0:T(8,128)S(1)}, u32[]{:S(2)}, u32[]{:S(2)}) collective-permute-start(f32[160,128]{1,0:T(8,128)S(1)} %add_add_fusion.1), channel_id=1, source_target_pairs={{0,2},{1,3},{2,0},{3,1},{4,6},{5,7},{6,4},{7,5},{8,10},{9,11},{10,... | collective-permute-start | bytes 245768 | tf_op jit(solution)/shard_map/ppermute | solution.py:371
  72.6 1.5 %collective-permute-start.16 = (f32[160,128]{1,0:T(8,128)S(1)}, f32[160,128]{1,0:T(8,128)S(1)}, u32[]{:S(2)}, u32[]{:S(2)}) collective-permute-start(f32[160,128]{1,0:T(8,128)S(1)} %add_add_fusion.1), channel_id=1, source_target_pairs={{0,3},{1,0},{2,1},{3,2},{4,7},{5,4},{6,5},{7,6},{8,11},{9,8},{10,9... | collective-permute-start | bytes 245768 | tf_op jit(solution)/shard_map/ppermute | solution.py:371
  74.5 1.4 %collective-permute-done.15 = f32[160,128]{1,0:T(8,128)S(1)} collective-permute-done((f32[160,128]{1,0:T(8,128)S(1)}, f32[160,128]{1,0:T(8,128)S(1)}, u32[]{:S(2)}, u32[]{:S(2)}) %collective-permute-start.15) | collective-permute-done | bytes 81952 | tf_op jit(solution)/shard_map/ppermute | solution.py:371
  76.1 2.7 %collective-permute-start.18 = (f32[160,128]{1,0:T(8,128)S(1)}, f32[160,128]{1,0:T(8,128)S(1)}, u32[]{:S(2)}, u32[]{:S(2)}) collective-permute-start(f32[160,128]{1,0:T(8,128)S(1)} %get-tuple-element.17), channel_id=1, source_target_pairs={{0,64},{32,96},{64,0},{96,32},{1,65},{33,97},{65,1},{97,33},{2,66}... | collective-permute-start | bytes 245768 | tf_op jit(solution)/shard_map/ppermute | solution.py:371
  78.8 1.7 %collective-permute-done.17 = f32[160,128]{1,0:T(8,128)S(1)} collective-permute-done((f32[160,128]{1,0:T(8,128)S(1)}, f32[160,128]{1,0:T(8,128)S(1)}, u32[]{:S(2)}, u32[]{:S(2)}) %collective-permute-start.17) | collective-permute-done | bytes 81952 | tf_op jit(solution)/shard_map/ppermute | solution.py:371
  82.1 6.2 %collective-permute-start.20 = (f32[640,128]{1,0:T(8,128)S(1)}, f32[640,128]{1,0:T(8,128)S(1)}, u32[]{:S(2)}, u32[]{:S(2)}) collective-permute-start(f32[640,128]{1,0:T(8,128)S(1)} %bitcast.27), channel_id=1, source_target_pairs={{0,4},{4,0},{1,5},{5,1},{2,6},{6,2},{3,7},{7,3},{8,12},{12,8},{9,1... | collective-permute-start | bytes 983048 | tf_op jit(solution)/shard_map/ppermute | solution.py:371
  89.5 21.6 %factor.1 = (f32[512,512]{1,0:T(8,128)}, f32[128,4096]{1,0:T(8,128)}) custom-call(s32[1]{0:T(128)} %bitcast.place, f32[640,128]{1,0:T(8,128)S(1)} %bitcast.28, f32[640,128]{1,0:T(8,128)S(1)} %collective-permute-done.20.other, f32[512,128]{1,0:T(8,128)S(1)} %copy-done.1, bf16[2,512,2048]{2,1,0:T(8,128)(2,1)} %get-tuple-element.12.cand_first, ...), custom_call_target="tpu_custom_call" | custom-call | tf_op jit(solution)/shard_map/factor/pallas_call | solution.py:345
  (47 shorter events, 11.3 us)
Async XLA Ops:
  2.2 28.8 %copy-start.2 = (f32[3,64,64]{2,1,0:T(8,128)S(1)}, f32[3,64,64]{2,1,0:T(8,128)}, u32[]{:S(2)}) copy-start(f32[3,64,64]{2,1,0:T(8,128)} %refs_8_.1) | copy-start | bytes 147460
  2.2 28.8 %copy-start.3 = (f32[3,64,64]{2,1,0:T(8,128)S(1)}, f32[3,64,64]{2,1,0:T(8,128)}, u32[]{:S(2)}) copy-start(f32[3,64,64]{2,1,0:T(8,128)} %refs_9_.1) | copy-start | bytes 147460
  2.2 19.1 %collective-permute-start = (f32[32,4096]{1,0:T(8,128)S(1)}, f32[32,4096]{1,0:T(8,128)S(1)}, u32[]{:S(2)}, u32[]{:S(2)}) collective-permute-start(f32[32,4096]{1,0:T(8,128)S(1)} %get-tuple-element.24), channel_id=1, source_target_pairs={{0,2},{1,3},{2,0},{3,1},{4,6},{5,7},{6,4},{7,5},{8,10},{9,11},{10,... | collective-permute-start | bytes 1572872 | tf_op jit(solution)/shard_map/ppermute | solution.py:371
  6.7 24.3 %collective-permute-start.1 = (f32[32,4096]{1,0:T(8,128)S(1)}, f32[32,4096]{1,0:T(8,128)S(1)}, u32[]{:S(2)}, u32[]{:S(2)}) collective-permute-start(f32[32,4096]{1,0:T(8,128)S(1)} %get-tuple-element.23), channel_id=1, source_target_pairs={{0,1},{1,2},{2,3},{3,0},{4,5},{5,6},{6,7},{7,4},{8,9},{9,10},{10,1... | collective-permute-start | bytes 1572872 | tf_op jit(solution)/shard_map/ppermute | solution.py:371
  7.4 23.6 %collective-permute-start.2 = (f32[32,4096]{1,0:T(8,128)S(1)}, f32[32,4096]{1,0:T(8,128)S(1)}, u32[]{:S(2)}, u32[]{:S(2)}) collective-permute-start(f32[32,4096]{1,0:T(8,128)S(1)} %get-tuple-element.22), channel_id=1, source_target_pairs={{0,3},{1,0},{2,1},{3,2},{4,7},{5,4},{6,5},{7,6},{8,11},{9,8},{10,9... | collective-permute-start | bytes 1572872 | tf_op jit(solution)/shard_map/ppermute | solution.py:371
  11.0 8.2 %collective-permute-start.3 = (f32[32,2048]{1,0:T(8,128)}, f32[32,2048]{1,0:T(8,128)}, u32[]{:S(2)}, u32[]{:S(2)}) collective-permute-start(f32[32,2048]{1,0:T(8,128)} %slice.10), channel_id=1, source_target_pairs={{0,4},{4,8},{8,12},{12,16},{16,20},{20,24},{24,28},{28,32},{32,36}... | collective-permute-start | bytes 786440 | tf_op jit(solution)/shard_map/ppermute | solution.py:421
  20.9 19.6 %collective-permute-start.4 = (f32[32,2048]{1,0:T(8,128)S(1)}, f32[32,2048]{1,0:T(8,128)S(1)}, u32[]{:S(2)}, u32[]{:S(2)}) collective-permute-start(f32[32,2048]{1,0:T(8,128)S(1)} %get-tuple-element.20), channel_id=1, source_target_pairs={{0,2},{1,3},{2,0},{3,1},{4,6},{5,7},{6,4},{7,5},{8,10},{9,11},{10,... | collective-permute-start | bytes 786440 | tf_op jit(solution)/shard_map/ppermute | solution.py:371
  21.0 20.6 %collective-permute-start.5 = (f32[32,2048]{1,0:T(8,128)S(1)}, f32[32,2048]{1,0:T(8,128)S(1)}, u32[]{:S(2)}, u32[]{:S(2)}) collective-permute-start(f32[32,2048]{1,0:T(8,128)S(1)} %get-tuple-element.19), channel_id=1, source_target_pairs={{0,1},{1,2},{2,3},{3,0},{4,5},{5,6},{6,7},{7,4},{8,9},{9,10},{10,1... | collective-permute-start | bytes 786440 | tf_op jit(solution)/shard_map/ppermute | solution.py:371
  21.3 20.3 %collective-permute-start.6 = (f32[32,2048]{1,0:T(8,128)S(1)}, f32[32,2048]{1,0:T(8,128)S(1)}, u32[]{:S(2)}, u32[]{:S(2)}) collective-permute-start(f32[32,2048]{1,0:T(8,128)S(1)} %get-tuple-element.18), channel_id=1, source_target_pairs={{0,3},{1,0},{2,1},{3,2},{4,7},{5,4},{6,5},{7,6},{8,11},{9,8},{10,9... | collective-permute-start | bytes 786440 | tf_op jit(solution)/shard_map/ppermute | solution.py:371
  50.1 39.4 %copy-start.1 = (f32[512,128]{1,0:T(8,128)S(1)}, f32[512,128]{1,0:T(8,128)}, u32[]{:S(2)}) copy-start(f32[512,128]{1,0:T(8,128)} %coeffs.1) | copy-start | bytes 786436
  50.1 2.6 %collective-permute-start.7 = (f32[640,128]{1,0:T(8,128)S(1)}, f32[640,128]{1,0:T(8,128)S(1)}, u32[]{:S(2)}, u32[]{:S(2)}) collective-permute-start(f32[640,128]{1,0:T(8,128)S(1)} %get-tuple-element.11), channel_id=1, source_target_pairs={{0,4},{4,0},{1,5},{5,1},{2,6},{6,2},{3,7},{7,3},{8,12},{12,8},{9,1... | collective-permute-start | bytes 983048 | tf_op jit(solution)/shard_map/ppermute | solution.py:371
  52.8 4.3 %collective-permute-start.10 = (f32[160,128]{1,0:T(8,128)S(1)}, f32[160,128]{1,0:T(8,128)S(1)}, u32[]{:S(2)}, u32[]{:S(2)}) collective-permute-start(f32[160,128]{1,0:T(8,128)S(1)} %get-tuple-element.26), channel_id=1, source_target_pairs={{0,96},{32,0},{64,32},{96,64},{1,97},{33,1},{65,33},{97,65},{2,98}... | collective-permute-start | bytes 245768 | tf_op jit(solution)/shard_map/ppermute | solution.py:371
  55.4 5.7 %collective-permute-start.8 = (f32[160,128]{1,0:T(8,128)S(1)}, f32[160,128]{1,0:T(8,128)S(1)}, u32[]{:S(2)}, u32[]{:S(2)}) collective-permute-start(f32[160,128]{1,0:T(8,128)S(1)} %get-tuple-element.25), channel_id=1, source_target_pairs={{0,32},{32,64},{64,96},{96,0},{1,33},{33,65},{65,97},{97,1},{2,34}... | collective-permute-start | bytes 245768 | tf_op jit(solution)/shard_map/ppermute | solution.py:371
  55.4 6.0 %collective-permute-start.9 = (f32[160,128]{1,0:T(8,128)S(1)}, f32[160,128]{1,0:T(8,128)S(1)}, u32[]{:S(2)}, u32[]{:S(2)}) collective-permute-start(f32[160,128]{1,0:T(8,128)S(1)} %get-tuple-element.27), channel_id=1, source_target_pairs={{0,64},{32,96},{64,0},{96,32},{1,65},{33,97},{65,1},{97,33},{2,66}... | collective-permute-start | bytes 245768 | tf_op jit(solution)/shard_map/ppermute | solution.py:371
  61.4 5.7 %collective-permute-start.11 = (f32[160,128]{1,0:T(8,128)S(1)}, f32[160,128]{1,0:T(8,128)S(1)}, u32[]{:S(2)}, u32[]{:S(2)}) collective-permute-start(f32[160,128]{1,0:T(8,128)S(1)} %fusion.1), channel_id=1, source_target_pairs={{0,16},{8,24},{16,0},{24,8},{1,17},{9,25},{17,1},{25,9},{2,18},{10... | collective-permute-start | bytes 245768 | tf_op jit(solution)/shard_map/ppermute | solution.py:371
  64.4 5.2 %collective-permute-start.12 = (f32[160,128]{1,0:T(8,128)S(1)}, f32[160,128]{1,0:T(8,128)S(1)}, u32[]{:S(2)}, u32[]{:S(2)}) collective-permute-start(f32[160,128]{1,0:T(8,128)S(1)} %fusion.1), channel_id=1, source_target_pairs={{0,8},{8,16},{16,24},{24,0},{1,9},{9,17},{17,25},{25,1},{2,10},{10... | collective-permute-start | bytes 245768 | tf_op jit(solution)/shard_map/ppermute | solution.py:371
  64.8 4.8 %collective-permute-start.13 = (f32[160,128]{1,0:T(8,128)S(1)}, f32[160,128]{1,0:T(8,128)S(1)}, u32[]{:S(2)}, u32[]{:S(2)}) collective-permute-start(f32[160,128]{1,0:T(8,128)S(1)} %fusion.1), channel_id=1, source_target_pairs={{0,24},{8,0},{16,8},{24,16},{1,25},{9,1},{17,9},{25,17},{2,26},{10... | collective-permute-start | bytes 245768 | tf_op jit(solution)/shard_map/ppermute | solution.py:371
  69.6 4.9 %collective-permute-start.14 = (f32[160,128]{1,0:T(8,128)S(1)}, f32[160,128]{1,0:T(8,128)S(1)}, u32[]{:S(2)}, u32[]{:S(2)}) collective-permute-start(f32[160,128]{1,0:T(8,128)S(1)} %add_add_fusion.1), channel_id=1, source_target_pairs={{0,2},{1,3},{2,0},{3,1},{4,6},{5,7},{6,4},{7,5},{8,10},{9,11},{10,... | collective-permute-start | bytes 245768 | tf_op jit(solution)/shard_map/ppermute | solution.py:371
  71.4 4.5 %collective-permute-start.15 = (f32[160,128]{1,0:T(8,128)S(1)}, f32[160,128]{1,0:T(8,128)S(1)}, u32[]{:S(2)}, u32[]{:S(2)}) collective-permute-start(f32[160,128]{1,0:T(8,128)S(1)} %add_add_fusion.1), channel_id=1, source_target_pairs={{0,1},{1,2},{2,3},{3,0},{4,5},{5,6},{6,7},{7,4},{8,9},{9,10},{10,1... | collective-permute-start | bytes 245768 | tf_op jit(solution)/shard_map/ppermute | solution.py:371
  72.6 3.3 %collective-permute-start.16 = (f32[160,128]{1,0:T(8,128)S(1)}, f32[160,128]{1,0:T(8,128)S(1)}, u32[]{:S(2)}, u32[]{:S(2)}) collective-permute-start(f32[160,128]{1,0:T(8,128)S(1)} %add_add_fusion.1), channel_id=1, source_target_pairs={{0,3},{1,0},{2,1},{3,2},{4,7},{5,4},{6,5},{7,6},{8,11},{9,8},{10,9... | collective-permute-start | bytes 245768 | tf_op jit(solution)/shard_map/ppermute | solution.py:371
  75.9 4.6 %collective-permute-start.17 = (f32[160,128]{1,0:T(8,128)S(1)}, f32[160,128]{1,0:T(8,128)S(1)}, u32[]{:S(2)}, u32[]{:S(2)}) collective-permute-start(f32[160,128]{1,0:T(8,128)S(1)} %get-tuple-element.17), channel_id=1, source_target_pairs={{0,32},{32,64},{64,96},{96,0},{1,33},{33,65},{65,97},{97,1},{2,34}... | collective-permute-start | bytes 245768 | tf_op jit(solution)/shard_map/ppermute | solution.py:371
  76.1 5.4 %collective-permute-start.18 = (f32[160,128]{1,0:T(8,128)S(1)}, f32[160,128]{1,0:T(8,128)S(1)}, u32[]{:S(2)}, u32[]{:S(2)}) collective-permute-start(f32[160,128]{1,0:T(8,128)S(1)} %get-tuple-element.17), channel_id=1, source_target_pairs={{0,64},{32,96},{64,0},{96,32},{1,65},{33,97},{65,1},{97,33},{2,66}... | collective-permute-start | bytes 245768 | tf_op jit(solution)/shard_map/ppermute | solution.py:371
  78.8 3.3 %collective-permute-start.19 = (f32[160,128]{1,0:T(8,128)S(1)}, f32[160,128]{1,0:T(8,128)S(1)}, u32[]{:S(2)}, u32[]{:S(2)}) collective-permute-start(f32[160,128]{1,0:T(8,128)S(1)} %get-tuple-element.17), channel_id=1, source_target_pairs={{0,96},{32,0},{64,32},{96,64},{1,97},{33,1},{65,33},{97,65},{2,98}... | collective-permute-start | bytes 245768 | tf_op jit(solution)/shard_map/ppermute | solution.py:371
  82.1 7.4 %collective-permute-start.20 = (f32[640,128]{1,0:T(8,128)S(1)}, f32[640,128]{1,0:T(8,128)S(1)}, u32[]{:S(2)}, u32[]{:S(2)}) collective-permute-start(f32[640,128]{1,0:T(8,128)S(1)} %bitcast.27), channel_id=1, source_target_pairs={{0,4},{4,0},{1,5},{5,1},{2,6},{6,2},{3,7},{7,3},{8,12},{12,8},{9,1... | collective-permute-start | bytes 983048 | tf_op jit(solution)/shard_map/ppermute | solution.py:371
  (2 other events, 15.9 us)

commit v3 on v2

--- a/solution.py
+++ b/solution.py
@@ -382,7 +382,8 @@
 
 def scattered_sum(value, axis):
     pieces = pieces_from_here(value, axis)
-    return sum((sent(pieces[by], axis, by) for by in range(1, len(pieces))), pieces[0])
+    two, one, three = (sent(pieces[by], axis, by) for by in (2, 1, 3))
+    return (pieces[0] + two) + (one + three)
 
 
 def exchanged_sum(value, axis):
@@ -393,7 +394,7 @@
 def gathered(value, axis):
     count, here = lax.axis_size(axis), lax.axis_index(axis)
     out = jnp.zeros((count, *value.shape), value.dtype)
-    for by in range(count):
+    for by in (0, 2, 1, 3):
         part = sent(value, axis, by) if by else value
         out = lax.dynamic_update_index_in_dim(out, part, (here - by) % count, 0)
     return out.reshape(-1, value.shape[-1])

time: 112 us -> 111 us (level)
  no operation moved by 1% of the time
where the time goes in v3:
time: 111 us
  Pallas kernels  38.7 us (35%)
  starting transfers between devices  38.3 us (35%)
  waiting for transfers between devices  26.3 us (24%)
  local copies, waits for them, and re-layouts  4.24 us (4%)
  other arithmetic  1.81 us (2%)
  between operations  1.12 us (1%)
    ppermute x20, starting transfers between devices, sent(): lax.ppermute(value, axis, [(i, (i + by) % count) for i in range(count)])  33.7 us
    ppermute x20, waiting for transfers between devices, sent(): lax.ppermute(value, axis, [(i, (i + by) % count) for i in range(count)])  23.1 us
    pallas_call x1, Pallas kernels, factored(): pl.pallas_call(factor_kernel, out_shape=(jax.ShapeDtypeStruct((512, 512),...  21.6 us
    pallas_call x2, Pallas kernels, transported(): pl.pallas_call(functools.partial(transport_kernel, second), out_shape=(*g...  17.2 us
    ppermute x1, starting transfers between devices, shards(): above = lax.ppermute(above, SPACE, [(i, i + 1) for i in range(count - 1)])  4.59 us
    ppermute x1, waiting for transfers between devices, shards(): above = lax.ppermute(above, SPACE, [(i, i + 1) for i in range(count - 1)])  3.25 us
  transfers between devices with their start and end apart: 21, of which 13 were waited for; matrix products, arithmetic and copies ran while one was open for 3% of the time, Pallas kernels for 8%

profile of v3, /device:TPU:1, one launch (start us, length us, event | category | flops | bytes accessed | tf_op | source)
XLA Modules:
  0.0 110.5 jit_solution(16128233300348657209)
XLA Ops:
  0.7 1.5 %constant_dynamic-slice_fusion = (f32[32,4096]{1,0:T(8,128)S(1)}, f32[32,4096]{1,0:T(8,128)S(1)}, f32[32,4096]{1,0:T(8,128)S(1)}) fusion(f32[32,16384]{1,0:T(8,128)} %xfactor.3, s32[]{:T(128)S(6)} %select_n.202, s32[]{:T(128)S(6)} %select_n.200, s32[]{:T(128)S(6)} %select_n.198), kind=kLoop, calls=%fused_computation.15 | loop fusion | bytes 3145740 | tf_op jit(solution)/shard_map/dynamic_slice | solution.py:427
  2.2 4.5 %collective-permute-start = (f32[32,4096]{1,0:T(8,128)S(1)}, f32[32,4096]{1,0:T(8,128)S(1)}, u32[]{:S(2)}, u32[]{:S(2)}) collective-permute-start(f32[32,4096]{1,0:T(8,128)S(1)} %get-tuple-element.24), channel_id=1, source_target_pairs={{0,2},{1,3},{2,0},{3,1},{4,6},{5,7},{6,4},{7,5},{8,10},{9,11},{10,... | collective-permute-start | bytes 1572872 | tf_op jit(solution)/shard_map/ppermute | solution.py:371
  7.4 1.9 %collective-permute-start.2 = (f32[32,4096]{1,0:T(8,128)S(1)}, f32[32,4096]{1,0:T(8,128)S(1)}, u32[]{:S(2)}, u32[]{:S(2)}) collective-permute-start(f32[32,4096]{1,0:T(8,128)S(1)} %get-tuple-element.22), channel_id=1, source_target_pairs={{0,3},{1,0},{2,1},{3,2},{4,7},{5,4},{6,5},{7,6},{8,11},{9,8},{10,9... | collective-permute-start | bytes 1572872 | tf_op jit(solution)/shard_map/ppermute | solution.py:371
  9.4 1.7 %slice.10 = f32[32,2048]{1,0:T(8,128)} slice(f32[32,16384]{1,0:T(8,128)} %xfactor.3), slice={[0:32], [14336:16384]} | slice | bytes 524288 | tf_op jit(solution)/shard_map/slice | solution.py:421
  11.0 4.6 %collective-permute-start.3 = (f32[32,2048]{1,0:T(8,128)}, f32[32,2048]{1,0:T(8,128)}, u32[]{:S(2)}, u32[]{:S(2)}) collective-permute-start(f32[32,2048]{1,0:T(8,128)} %slice.10), channel_id=1, source_target_pairs={{0,4},{4,8},{8,12},{12,16},{16,20},{20,24},{24,28},{28,32},{32,36}... | collective-permute-start | bytes 786440 | tf_op jit(solution)/shard_map/ppermute | solution.py:422
  16.0 3.3 %collective-permute-done.3 = f32[32,2048]{1,0:T(8,128)} collective-permute-done((f32[32,2048]{1,0:T(8,128)}, f32[32,2048]{1,0:T(8,128)}, u32[]{:S(2)}, u32[]{:S(2)}) %collective-permute-start.3) | collective-permute-done | bytes 262176 | tf_op jit(solution)/shard_map/ppermute | solution.py:422
  19.3 1.6 %dynamic-slice_select_fusion = (f32[32,2048]{1,0:T(8,128)S(1)}, f32[32,2048]{1,0:T(8,128)S(1)}, f32[32,2048]{1,0:T(8,128)S(1)}, f32[32,2048]{1,0:T(8,128)S(1)}) fusion(f32[32,2048]{1,0:T(8,128)} %collective-permute-done.3, f32[32,16384]{1,0:T(8,128)} %xfactor.3, s32[]{:T(128)S(6)} %max.15, pred[]{:T(512)S(6)} %eq.59, s32[]{:T(128)S(6)} %max.14, pred[]{:T(512)S(6)} %eq.58, ...), kind=kLoop, calls=%fused_computation | loop fusion | flops 262144 | bytes 2359316 | tf_op jit(solution)/shard_map/jit(_where)/select_n | solution.py:432
  21.3 2.5 %collective-permute-start.6 = (f32[32,2048]{1,0:T(8,128)S(1)}, f32[32,2048]{1,0:T(8,128)S(1)}, u32[]{:S(2)}, u32[]{:S(2)}) collective-permute-start(f32[32,2048]{1,0:T(8,128)S(1)} %get-tuple-element.18), channel_id=1, source_target_pairs={{0,3},{1,0},{2,1},{3,2},{4,7},{5,4},{6,5},{7,6},{8,11},{9,8},{10,9... | collective-permute-start | bytes 786440 | tf_op jit(solution)/shard_map/ppermute | solution.py:371
  23.7 7.3 %collective-permute-done.1.refs_1_ = f32[32,4096]{1,0:T(8,128)S(1)} collective-permute-done((f32[32,4096]{1,0:T(8,128)S(1)}, f32[32,4096]{1,0:T(8,128)S(1)}, u32[]{:S(2)}, u32[]{:S(2)}) %collective-permute-start.1) | collective-permute-done | bytes 524320 | tf_op jit(solution)/shard_map/ppermute | solution.py:371
  31.0 8.6 %transport_second.1 = (f32[1280,128]{1,0:T(8,128)S(1)}, bf16[2,512,2048]{2,1,0:T(8,128)(2,1)}) custom-call(s32[5]{0:T(128)S(1)} %stack.23.place, s32[3,32]{1,0:T(4,128)S(1)} %get-tuple-element.28.index, f32[32,16384]{1,0:T(8,128)} %xfactor.3, f32[32,4096]{1,0:T(8,128)S(1)} %collective-permute-done.refs_0_, f32[32,4096]{1,0:T(8,128)S(1)} %collective-permute-done.1.refs_1_, ...), custom_call_target="tpu_custom_call" | custom-call | flops 8999999488 | bytes 8388608 | tf_op jit(solution)/shard_map/transport_second/pallas_call | solution.py:181
  41.6 8.5 %transport_first.1 = (f32[640,128]{1,0:T(8,128)S(1)}, f32[640,128]{1,0:T(8,128)S(1)}, bf16[2,512,2048]{2,1,0:T(8,128)(2,1)}) custom-call(s32[5]{0:T(128)S(1)} %stack.23.place, s32[3,32]{1,0:T(4,128)S(1)} %get-tuple-element.29.index, f32[32,16384]{1,0:T(8,128)} %xfactor.3, f32[32,4096]{1,0:T(8,128)S(1)} %collective-permute-done.refs_0_, ...), custom_call_target="tpu_custom_call" | custom-call | flops 8999999488 | bytes 8388608 | tf_op jit(solution)/shard_map/transport_first/pallas_call | solution.py:181
  52.8 2.5 %collective-permute-start.10 = (f32[160,128]{1,0:T(8,128)S(1)}, f32[160,128]{1,0:T(8,128)S(1)}, u32[]{:S(2)}, u32[]{:S(2)}) collective-permute-start(f32[160,128]{1,0:T(8,128)S(1)} %get-tuple-element.25), channel_id=1, source_target_pairs={{0,96},{32,0},{64,32},{96,64},{1,97},{33,1},{65,33},{97,65},{2,98}... | collective-permute-start | bytes 245768 | tf_op jit(solution)/shard_map/ppermute | solution.py:371
  56.9 3.4 %collective-permute-done.8 = f32[160,128]{1,0:T(8,128)S(1)} collective-permute-done((f32[160,128]{1,0:T(8,128)S(1)}, f32[160,128]{1,0:T(8,128)S(1)}, u32[]{:S(2)}, u32[]{:S(2)}) %collective-permute-start.8) | collective-permute-done | bytes 81952 | tf_op jit(solution)/shard_map/ppermute | solution.py:371
  60.2 2.3 %collective-permute-done.9 = f32[160,128]{1,0:T(8,128)S(1)} collective-permute-done((f32[160,128]{1,0:T(8,128)S(1)}, f32[160,128]{1,0:T(8,128)S(1)}, u32[]{:S(2)}, u32[]{:S(2)}) %collective-permute-start.9) | collective-permute-done | bytes 81952 | tf_op jit(solution)/shard_map/ppermute | solution.py:371
  62.6 3.0 %collective-permute-start.11 = (f32[160,128]{1,0:T(8,128)S(1)}, f32[160,128]{1,0:T(8,128)S(1)}, u32[]{:S(2)}, u32[]{:S(2)}) collective-permute-start(f32[160,128]{1,0:T(8,128)S(1)} %fusion), channel_id=1, source_target_pairs={{0,16},{8,24},{16,0},{24,8},{1,17},{9,25},{17,1},{25,9},{2,18},{10... | collective-permute-start | bytes 245768 | tf_op jit(solution)/shard_map/ppermute | solution.py:371
  66.0 2.3 %collective-permute-start.13 = (f32[160,128]{1,0:T(8,128)S(1)}, f32[160,128]{1,0:T(8,128)S(1)}, u32[]{:S(2)}, u32[]{:S(2)}) collective-permute-start(f32[160,128]{1,0:T(8,128)S(1)} %fusion), channel_id=1, source_target_pairs={{0,24},{8,0},{16,8},{24,16},{1,25},{9,1},{17,9},{25,17},{2,26},{10... | collective-permute-start | bytes 245768 | tf_op jit(solution)/shard_map/ppermute | solution.py:371
  68.3 1.9 %collective-permute-done.12 = f32[160,128]{1,0:T(8,128)S(1)} collective-permute-done((f32[160,128]{1,0:T(8,128)S(1)}, f32[160,128]{1,0:T(8,128)S(1)}, u32[]{:S(2)}, u32[]{:S(2)}) %collective-permute-start.12) | collective-permute-done | bytes 81952 | tf_op jit(solution)/shard_map/ppermute | solution.py:371
  70.2 1.8 %collective-permute-start.14 = (f32[160,128]{1,0:T(8,128)S(1)}, f32[160,128]{1,0:T(8,128)S(1)}, u32[]{:S(2)}, u32[]{:S(2)}) collective-permute-start(f32[160,128]{1,0:T(8,128)S(1)} %add_add_fusion.1), channel_id=1, source_target_pairs={{0,2},{1,3},{2,0},{3,1},{4,6},{5,7},{6,4},{7,5},{8,10},{9,11},{10,... | collective-permute-start | bytes 245768 | tf_op jit(solution)/shard_map/ppermute | solution.py:371
  73.1 1.5 %collective-permute-start.16 = (f32[160,128]{1,0:T(8,128)S(1)}, f32[160,128]{1,0:T(8,128)S(1)}, u32[]{:S(2)}, u32[]{:S(2)}) collective-permute-start(f32[160,128]{1,0:T(8,128)S(1)} %add_add_fusion.1), channel_id=1, source_target_pairs={{0,3},{1,0},{2,1},{3,2},{4,7},{5,4},{6,5},{7,6},{8,11},{9,8},{10,9... | collective-permute-start | bytes 245768 | tf_op jit(solution)/shard_map/ppermute | solution.py:371
  75.0 1.4 %collective-permute-done.15 = f32[160,128]{1,0:T(8,128)S(1)} collective-permute-done((f32[160,128]{1,0:T(8,128)S(1)}, f32[160,128]{1,0:T(8,128)S(1)}, u32[]{:S(2)}, u32[]{:S(2)}) %collective-permute-start.15) | collective-permute-done | bytes 81952 | tf_op jit(solution)/shard_map/ppermute | solution.py:371
  77.4 2.4 %collective-permute-start.19 = (f32[160,128]{1,0:T(8,128)S(1)}, f32[160,128]{1,0:T(8,128)S(1)}, u32[]{:S(2)}, u32[]{:S(2)}) collective-permute-start(f32[160,128]{1,0:T(8,128)S(1)} %get-tuple-element.17), channel_id=1, source_target_pairs={{0,96},{32,0},{64,32},{96,64},{1,97},{33,1},{65,33},{97,65},{2,98}... | collective-permute-start | bytes 245768 | tf_op jit(solution)/shard_map/ppermute | solution.py:371
  79.8 1.6 %collective-permute-done.17 = f32[160,128]{1,0:T(8,128)S(1)} collective-permute-done((f32[160,128]{1,0:T(8,128)S(1)}, f32[160,128]{1,0:T(8,128)S(1)}, u32[]{:S(2)}, u32[]{:S(2)}) %collective-permute-start.17) | collective-permute-done | bytes 81952 | tf_op jit(solution)/shard_map/ppermute | solution.py:371
  82.3 5.2 %collective-permute-start.20 = (f32[640,128]{1,0:T(8,128)S(1)}, f32[640,128]{1,0:T(8,128)S(1)}, u32[]{:S(2)}, u32[]{:S(2)}) collective-permute-start(f32[640,128]{1,0:T(8,128)S(1)} %bitcast.25), channel_id=1, source_target_pairs={{0,4},{4,0},{1,5},{5,1},{2,6},{6,2},{3,7},{7,3},{8,12},{12,8},{9,1... | collective-permute-start | bytes 983048 | tf_op jit(solution)/shard_map/ppermute | solution.py:371
  88.8 21.6 %factor.1 = (f32[512,512]{1,0:T(8,128)}, f32[128,4096]{1,0:T(8,128)}) custom-call(s32[1]{0:T(128)} %bitcast.place, f32[640,128]{1,0:T(8,128)S(1)} %bitcast.26, f32[640,128]{1,0:T(8,128)S(1)} %collective-permute-done.20.other, f32[512,128]{1,0:T(8,128)S(1)} %copy-done.1, bf16[2,512,2048]{2,1,0:T(8,128)(2,1)} %get-tuple-element.12.cand_first, ...), custom_call_target="tpu_custom_call" | custom-call | tf_op jit(solution)/shard_map/factor/pallas_call | solution.py:345
  (47 shorter events, 12.5 us)
Async XLA Ops:
  2.2 28.8 %copy-start.2 = (f32[3,64,64]{2,1,0:T(8,128)S(1)}, f32[3,64,64]{2,1,0:T(8,128)}, u32[]{:S(2)}) copy-start(f32[3,64,64]{2,1,0:T(8,128)} %refs_8_.1) | copy-start | bytes 147460
  2.2 28.8 %copy-start.3 = (f32[3,64,64]{2,1,0:T(8,128)S(1)}, f32[3,64,64]{2,1,0:T(8,128)}, u32[]{:S(2)}) copy-start(f32[3,64,64]{2,1,0:T(8,128)} %refs_9_.1) | copy-start | bytes 147460
  2.2 19.1 %collective-permute-start = (f32[32,4096]{1,0:T(8,128)S(1)}, f32[32,4096]{1,0:T(8,128)S(1)}, u32[]{:S(2)}, u32[]{:S(2)}) collective-permute-start(f32[32,4096]{1,0:T(8,128)S(1)} %get-tuple-element.24), channel_id=1, source_target_pairs={{0,2},{1,3},{2,0},{3,1},{4,6},{5,7},{6,4},{7,5},{8,10},{9,11},{10,... | collective-permute-start | bytes 1572872 | tf_op jit(solution)/shard_map/ppermute | solution.py:371
  6.7 24.3 %collective-permute-start.1 = (f32[32,4096]{1,0:T(8,128)S(1)}, f32[32,4096]{1,0:T(8,128)S(1)}, u32[]{:S(2)}, u32[]{:S(2)}) collective-permute-start(f32[32,4096]{1,0:T(8,128)S(1)} %get-tuple-element.23), channel_id=1, source_target_pairs={{0,1},{1,2},{2,3},{3,0},{4,5},{5,6},{6,7},{7,4},{8,9},{9,10},{10,1... | collective-permute-start | bytes 1572872 | tf_op jit(solution)/shard_map/ppermute | solution.py:371
  7.4 23.6 %collective-permute-start.2 = (f32[32,4096]{1,0:T(8,128)S(1)}, f32[32,4096]{1,0:T(8,128)S(1)}, u32[]{:S(2)}, u32[]{:S(2)}) collective-permute-start(f32[32,4096]{1,0:T(8,128)S(1)} %get-tuple-element.22), channel_id=1, source_target_pairs={{0,3},{1,0},{2,1},{3,2},{4,7},{5,4},{6,5},{7,6},{8,11},{9,8},{10,9... | collective-permute-start | bytes 1572872 | tf_op jit(solution)/shard_map/ppermute | solution.py:371
  11.0 8.2 %collective-permute-start.3 = (f32[32,2048]{1,0:T(8,128)}, f32[32,2048]{1,0:T(8,128)}, u32[]{:S(2)}, u32[]{:S(2)}) collective-permute-start(f32[32,2048]{1,0:T(8,128)} %slice.10), channel_id=1, source_target_pairs={{0,4},{4,8},{8,12},{12,16},{16,20},{20,24},{24,28},{28,32},{32,36}... | collective-permute-start | bytes 786440 | tf_op jit(solution)/shard_map/ppermute | solution.py:422
  20.9 19.6 %collective-permute-start.4 = (f32[32,2048]{1,0:T(8,128)S(1)}, f32[32,2048]{1,0:T(8,128)S(1)}, u32[]{:S(2)}, u32[]{:S(2)}) collective-permute-start(f32[32,2048]{1,0:T(8,128)S(1)} %get-tuple-element.20), channel_id=1, source_target_pairs={{0,2},{1,3},{2,0},{3,1},{4,6},{5,7},{6,4},{7,5},{8,10},{9,11},{10,... | collective-permute-start | bytes 786440 | tf_op jit(solution)/shard_map/ppermute | solution.py:371
  21.0 20.6 %collective-permute-start.5 = (f32[32,2048]{1,0:T(8,128)S(1)}, f32[32,2048]{1,0:T(8,128)S(1)}, u32[]{:S(2)}, u32[]{:S(2)}) collective-permute-start(f32[32,2048]{1,0:T(8,128)S(1)} %get-tuple-element.19), channel_id=1, source_target_pairs={{0,1},{1,2},{2,3},{3,0},{4,5},{5,6},{6,7},{7,4},{8,9},{9,10},{10,1... | collective-permute-start | bytes 786440 | tf_op jit(solution)/shard_map/ppermute | solution.py:371
  21.3 20.3 %collective-permute-start.6 = (f32[32,2048]{1,0:T(8,128)S(1)}, f32[32,2048]{1,0:T(8,128)S(1)}, u32[]{:S(2)}, u32[]{:S(2)}) collective-permute-start(f32[32,2048]{1,0:T(8,128)S(1)} %get-tuple-element.18), channel_id=1, source_target_pairs={{0,3},{1,0},{2,1},{3,2},{4,7},{5,4},{6,5},{7,6},{8,11},{9,8},{10,9... | collective-permute-start | bytes 786440 | tf_op jit(solution)/shard_map/ppermute | solution.py:371
  50.1 38.7 %copy-start.1 = (f32[512,128]{1,0:T(8,128)S(1)}, f32[512,128]{1,0:T(8,128)}, u32[]{:S(2)}) copy-start(f32[512,128]{1,0:T(8,128)} %coeffs.1) | copy-start | bytes 786436
  50.1 2.6 %collective-permute-start.7 = (f32[640,128]{1,0:T(8,128)S(1)}, f32[640,128]{1,0:T(8,128)S(1)}, u32[]{:S(2)}, u32[]{:S(2)}) collective-permute-start(f32[640,128]{1,0:T(8,128)S(1)} %get-tuple-element.11), channel_id=1, source_target_pairs={{0,4},{4,0},{1,5},{5,1},{2,6},{6,2},{3,7},{7,3},{8,12},{12,8},{9,1... | collective-permute-start | bytes 983048 | tf_op jit(solution)/shard_map/ppermute | solution.py:371
  52.8 4.0 %collective-permute-start.10 = (f32[160,128]{1,0:T(8,128)S(1)}, f32[160,128]{1,0:T(8,128)S(1)}, u32[]{:S(2)}, u32[]{:S(2)}) collective-permute-start(f32[160,128]{1,0:T(8,128)S(1)} %get-tuple-element.25), channel_id=1, source_target_pairs={{0,96},{32,0},{64,32},{96,64},{1,97},{33,1},{65,33},{97,65},{2,98}... | collective-permute-start | bytes 245768 | tf_op jit(solution)/shard_map/ppermute | solution.py:371
  55.4 4.9 %collective-permute-start.8 = (f32[160,128]{1,0:T(8,128)S(1)}, f32[160,128]{1,0:T(8,128)S(1)}, u32[]{:S(2)}, u32[]{:S(2)}) collective-permute-start(f32[160,128]{1,0:T(8,128)S(1)} %get-tuple-element.27), channel_id=1, source_target_pairs={{0,64},{32,96},{64,0},{96,32},{1,65},{33,97},{65,1},{97,33},{2,66}... | collective-permute-start | bytes 245768 | tf_op jit(solution)/shard_map/ppermute | solution.py:371
  56.0 6.6 %collective-permute-start.9 = (f32[160,128]{1,0:T(8,128)S(1)}, f32[160,128]{1,0:T(8,128)S(1)}, u32[]{:S(2)}, u32[]{:S(2)}) collective-permute-start(f32[160,128]{1,0:T(8,128)S(1)} %get-tuple-element.26), channel_id=1, source_target_pairs={{0,32},{32,64},{64,96},{96,0},{1,33},{33,65},{65,97},{97,1},{2,34}... | collective-permute-start | bytes 245768 | tf_op jit(solution)/shard_map/ppermute | solution.py:371
  62.6 5.7 %collective-permute-start.11 = (f32[160,128]{1,0:T(8,128)S(1)}, f32[160,128]{1,0:T(8,128)S(1)}, u32[]{:S(2)}, u32[]{:S(2)}) collective-permute-start(f32[160,128]{1,0:T(8,128)S(1)} %fusion), channel_id=1, source_target_pairs={{0,16},{8,24},{16,0},{24,8},{1,17},{9,25},{17,1},{25,9},{2,18},{10... | collective-permute-start | bytes 245768 | tf_op jit(solution)/shard_map/ppermute | solution.py:371
  65.6 4.5 %collective-permute-start.12 = (f32[160,128]{1,0:T(8,128)S(1)}, f32[160,128]{1,0:T(8,128)S(1)}, u32[]{:S(2)}, u32[]{:S(2)}) collective-permute-start(f32[160,128]{1,0:T(8,128)S(1)} %fusion), channel_id=1, source_target_pairs={{0,8},{8,16},{16,24},{24,0},{1,9},{9,17},{17,25},{25,1},{2,10},{10... | collective-permute-start | bytes 245768 | tf_op jit(solution)/shard_map/ppermute | solution.py:371
  66.0 4.2 %collective-permute-start.13 = (f32[160,128]{1,0:T(8,128)S(1)}, f32[160,128]{1,0:T(8,128)S(1)}, u32[]{:S(2)}, u32[]{:S(2)}) collective-permute-start(f32[160,128]{1,0:T(8,128)S(1)} %fusion), channel_id=1, source_target_pairs={{0,24},{8,0},{16,8},{24,16},{1,25},{9,1},{17,9},{25,17},{2,26},{10... | collective-permute-start | bytes 245768 | tf_op jit(solution)/shard_map/ppermute | solution.py:371
  70.2 4.9 %collective-permute-start.14 = (f32[160,128]{1,0:T(8,128)S(1)}, f32[160,128]{1,0:T(8,128)S(1)}, u32[]{:S(2)}, u32[]{:S(2)}) collective-permute-start(f32[160,128]{1,0:T(8,128)S(1)} %add_add_fusion.1), channel_id=1, source_target_pairs={{0,2},{1,3},{2,0},{3,1},{4,6},{5,7},{6,4},{7,5},{8,10},{9,11},{10,... | collective-permute-start | bytes 245768 | tf_op jit(solution)/shard_map/ppermute | solution.py:371
  72.0 4.5 %collective-permute-start.15 = (f32[160,128]{1,0:T(8,128)S(1)}, f32[160,128]{1,0:T(8,128)S(1)}, u32[]{:S(2)}, u32[]{:S(2)}) collective-permute-start(f32[160,128]{1,0:T(8,128)S(1)} %add_add_fusion.1), channel_id=1, source_target_pairs={{0,1},{1,2},{2,3},{3,0},{4,5},{5,6},{6,7},{7,4},{8,9},{9,10},{10,1... | collective-permute-start | bytes 245768 | tf_op jit(solution)/shard_map/ppermute | solution.py:371
  73.1 3.3 %collective-permute-start.16 = (f32[160,128]{1,0:T(8,128)S(1)}, f32[160,128]{1,0:T(8,128)S(1)}, u32[]{:S(2)}, u32[]{:S(2)}) collective-permute-start(f32[160,128]{1,0:T(8,128)S(1)} %add_add_fusion.1), channel_id=1, source_target_pairs={{0,3},{1,0},{2,1},{3,2},{4,7},{5,4},{6,5},{7,6},{8,11},{9,8},{10,9... | collective-permute-start | bytes 245768 | tf_op jit(solution)/shard_map/ppermute | solution.py:371
  76.5 4.9 %collective-permute-start.17 = (f32[160,128]{1,0:T(8,128)S(1)}, f32[160,128]{1,0:T(8,128)S(1)}, u32[]{:S(2)}, u32[]{:S(2)}) collective-permute-start(f32[160,128]{1,0:T(8,128)S(1)} %get-tuple-element.17), channel_id=1, source_target_pairs={{0,64},{32,96},{64,0},{96,32},{1,65},{33,97},{65,1},{97,33},{2,66}... | collective-permute-start | bytes 245768 | tf_op jit(solution)/shard_map/ppermute | solution.py:371
  77.1 5.1 %collective-permute-start.18 = (f32[160,128]{1,0:T(8,128)S(1)}, f32[160,128]{1,0:T(8,128)S(1)}, u32[]{:S(2)}, u32[]{:S(2)}) collective-permute-start(f32[160,128]{1,0:T(8,128)S(1)} %get-tuple-element.17), channel_id=1, source_target_pairs={{0,32},{32,64},{64,96},{96,0},{1,33},{33,65},{65,97},{97,1},{2,34}... | collective-permute-start | bytes 245768 | tf_op jit(solution)/shard_map/ppermute | solution.py:371
  77.4 4.9 %collective-permute-start.19 = (f32[160,128]{1,0:T(8,128)S(1)}, f32[160,128]{1,0:T(8,128)S(1)}, u32[]{:S(2)}, u32[]{:S(2)}) collective-permute-start(f32[160,128]{1,0:T(8,128)S(1)} %get-tuple-element.17), channel_id=1, source_target_pairs={{0,96},{32,0},{64,32},{96,64},{1,97},{33,1},{65,33},{97,65},{2,98}... | collective-permute-start | bytes 245768 | tf_op jit(solution)/shard_map/ppermute | solution.py:371
  82.3 6.5 %collective-permute-start.20 = (f32[640,128]{1,0:T(8,128)S(1)}, f32[640,128]{1,0:T(8,128)S(1)}, u32[]{:S(2)}, u32[]{:S(2)}) collective-permute-start(f32[640,128]{1,0:T(8,128)S(1)} %bitcast.25), channel_id=1, source_target_pairs={{0,4},{4,0},{1,5},{5,1},{2,6},{6,2},{3,7},{7,3},{8,12},{12,8},{9,1... | collective-permute-start | bytes 983048 | tf_op jit(solution)/shard_map/ppermute | solution.py:371
  (2 other events, 15.9 us)

commit v4 on v3

--- a/solution.py
+++ b/solution.py
@@ -387,14 +387,14 @@
 
 
 def exchanged_sum(value, axis):
-    one, two, three = (sent(value, axis, by) for by in range(1, 4))
-    return (value + two) + (one + three)
+    three, two, one = (sent(value, axis, by) for by in (3, 2, 1))
+    return (three + one) + (two + value)
 
 
 def gathered(value, axis):
     count, here = lax.axis_size(axis), lax.axis_index(axis)
     out = jnp.zeros((count, *value.shape), value.dtype)
-    for by in (0, 2, 1, 3):
+    for by in (0, 3, 2, 1):
         part = sent(value, axis, by) if by else value
         out = lax.dynamic_update_index_in_dim(out, part, (here - by) % count, 0)
     return out.reshape(-1, value.shape[-1])

time: 111 us -> 113 us (1.018)
  waiting for transfers between devices: 26.3 us -> 32.4 us
  starting transfers between devices: 38.3 us -> 34.6 us
    ppermute x20, waiting for transfers between devices: 23.1 us -> 29.1 us  [sent(): lax.ppermute(value, axis, [(i, (i + by) % count) for i in range(count)])]
    ppermute x20, starting transfers between devices: 33.7 us -> 30 us  [sent(): lax.ppermute(value, axis, [(i, (i + by) % count) for i in range(count)])]
  transfers between devices with their start and end apart: 21 -> 21, of which waited for: 13 -> 15; matrix products, arithmetic and copies ran while one was open for 3% -> 3% of each run, Pallas kernels for 8% -> 8%
where the time goes in v4:
time: 113 us
  Pallas kernels  38.7 us (34%)
  starting transfers between devices  34.6 us (31%)
  waiting for transfers between devices  32.4 us (29%)
  local copies, waits for them, and re-layouts  4.24 us (4%)
  other arithmetic  1.82 us (2%)
  between operations  1.18 us (1%)
    ppermute x20, starting transfers between devices, sent(): lax.ppermute(value, axis, [(i, (i + by) % count) for i in range(count)])  30 us
    ppermute x20, waiting for transfers between devices, sent(): lax.ppermute(value, axis, [(i, (i + by) % count) for i in range(count)])  29.1 us
    pallas_call x1, Pallas kernels, factored(): pl.pallas_call(factor_kernel, out_shape=(jax.ShapeDtypeStruct((512, 512),...  21.6 us
    pallas_call x2, Pallas kernels, transported(): pl.pallas_call(functools.partial(transport_kernel, second), out_shape=(*g...  17.2 us
    ppermute x1, starting transfers between devices, shards(): above = lax.ppermute(above, SPACE, [(i, i + 1) for i in range(count - 1)])  4.59 us
    ppermute x1, waiting for transfers between devices, shards(): above = lax.ppermute(above, SPACE, [(i, i + 1) for i in range(count - 1)])  3.25 us
  transfers between devices with their start and end apart: 21, of which 15 were waited for; matrix products, arithmetic and copies ran while one was open for 3% of the time, Pallas kernels for 8%

profile of v4, /device:TPU:1, one launch (start us, length us, event | category | flops | bytes accessed | tf_op | source)
XLA Modules:
  0.0 113.0 jit_solution(9446732905825779634)
XLA Ops:
  0.7 1.5 %constant_dynamic-slice_fusion = (f32[32,4096]{1,0:T(8,128)S(1)}, f32[32,4096]{1,0:T(8,128)S(1)}, f32[32,4096]{1,0:T(8,128)S(1)}) fusion(f32[32,16384]{1,0:T(8,128)} %xfactor.3, s32[]{:T(128)S(6)} %select_n.202, s32[]{:T(128)S(6)} %select_n.200, s32[]{:T(128)S(6)} %select_n.198), kind=kLoop, calls=%fused_computation.15 | loop fusion | bytes 3145740 | tf_op jit(solution)/shard_map/dynamic_slice | solution.py:427
  2.2 4.5 %collective-permute-start = (f32[32,4096]{1,0:T(8,128)S(1)}, f32[32,4096]{1,0:T(8,128)S(1)}, u32[]{:S(2)}, u32[]{:S(2)}) collective-permute-start(f32[32,4096]{1,0:T(8,128)S(1)} %get-tuple-element.24), channel_id=1, source_target_pairs={{0,2},{1,3},{2,0},{3,1},{4,6},{5,7},{6,4},{7,5},{8,10},{9,11},{10,... | collective-permute-start | bytes 1572872 | tf_op jit(solution)/shard_map/ppermute | solution.py:371
  7.4 1.9 %collective-permute-start.2 = (f32[32,4096]{1,0:T(8,128)S(1)}, f32[32,4096]{1,0:T(8,128)S(1)}, u32[]{:S(2)}, u32[]{:S(2)}) collective-permute-start(f32[32,4096]{1,0:T(8,128)S(1)} %get-tuple-element.22), channel_id=1, source_target_pairs={{0,3},{1,0},{2,1},{3,2},{4,7},{5,4},{6,5},{7,6},{8,11},{9,8},{10,9... | collective-permute-start | bytes 1572872 | tf_op jit(solution)/shard_map/ppermute | solution.py:371
  9.4 1.7 %slice.10 = f32[32,2048]{1,0:T(8,128)} slice(f32[32,16384]{1,0:T(8,128)} %xfactor.3), slice={[0:32], [14336:16384]} | slice | bytes 524288 | tf_op jit(solution)/shard_map/slice | solution.py:421
  11.0 4.6 %collective-permute-start.3 = (f32[32,2048]{1,0:T(8,128)}, f32[32,2048]{1,0:T(8,128)}, u32[]{:S(2)}, u32[]{:S(2)}) collective-permute-start(f32[32,2048]{1,0:T(8,128)} %slice.10), channel_id=1, source_target_pairs={{0,4},{4,8},{8,12},{12,16},{16,20},{20,24},{24,28},{28,32},{32,36}... | collective-permute-start | bytes 786440 | tf_op jit(solution)/shard_map/ppermute | solution.py:422
  16.0 3.3 %collective-permute-done.3 = f32[32,2048]{1,0:T(8,128)} collective-permute-done((f32[32,2048]{1,0:T(8,128)}, f32[32,2048]{1,0:T(8,128)}, u32[]{:S(2)}, u32[]{:S(2)}) %collective-permute-start.3) | collective-permute-done | bytes 262176 | tf_op jit(solution)/shard_map/ppermute | solution.py:422
  19.3 1.6 %dynamic-slice_select_fusion = (f32[32,2048]{1,0:T(8,128)S(1)}, f32[32,2048]{1,0:T(8,128)S(1)}, f32[32,2048]{1,0:T(8,128)S(1)}, f32[32,2048]{1,0:T(8,128)S(1)}) fusion(f32[32,2048]{1,0:T(8,128)} %collective-permute-done.3, f32[32,16384]{1,0:T(8,128)} %xfactor.3, s32[]{:T(128)S(6)} %max.15, pred[]{:T(512)S(6)} %eq.59, s32[]{:T(128)S(6)} %max.14, pred[]{:T(512)S(6)} %eq.58, ...), kind=kLoop, calls=%fused_computation | loop fusion | flops 262144 | bytes 2359316 | tf_op jit(solution)/shard_map/jit(_where)/select_n | solution.py:432
  21.3 2.5 %collective-permute-start.6 = (f32[32,2048]{1,0:T(8,128)S(1)}, f32[32,2048]{1,0:T(8,128)S(1)}, u32[]{:S(2)}, u32[]{:S(2)}) collective-permute-start(f32[32,2048]{1,0:T(8,128)S(1)} %get-tuple-element.18), channel_id=1, source_target_pairs={{0,3},{1,0},{2,1},{3,2},{4,7},{5,4},{6,5},{7,6},{8,11},{9,8},{10,9... | collective-permute-start | bytes 786440 | tf_op jit(solution)/shard_map/ppermute | solution.py:371
  23.7 7.3 %collective-permute-done.1.refs_1_ = f32[32,4096]{1,0:T(8,128)S(1)} collective-permute-done((f32[32,4096]{1,0:T(8,128)S(1)}, f32[32,4096]{1,0:T(8,128)S(1)}, u32[]{:S(2)}, u32[]{:S(2)}) %collective-permute-start.1) | collective-permute-done | bytes 524320 | tf_op jit(solution)/shard_map/ppermute | solution.py:371
  31.0 8.6 %transport_second.1 = (f32[1280,128]{1,0:T(8,128)S(1)}, bf16[2,512,2048]{2,1,0:T(8,128)(2,1)}) custom-call(s32[5]{0:T(128)S(1)} %stack.23.place, s32[3,32]{1,0:T(4,128)S(1)} %get-tuple-element.28.index, f32[32,16384]{1,0:T(8,128)} %xfactor.3, f32[32,4096]{1,0:T(8,128)S(1)} %collective-permute-done.refs_0_, f32[32,4096]{1,0:T(8,128)S(1)} %collective-permute-done.1.refs_1_, ...), custom_call_target="tpu_custom_call" | custom-call | flops 8999999488 | bytes 8388608 | tf_op jit(solution)/shard_map/transport_second/pallas_call | solution.py:181
  41.6 8.5 %transport_first.1 = (f32[640,128]{1,0:T(8,128)S(1)}, f32[640,128]{1,0:T(8,128)S(1)}, bf16[2,512,2048]{2,1,0:T(8,128)(2,1)}) custom-call(s32[5]{0:T(128)S(1)} %stack.23.place, s32[3,32]{1,0:T(4,128)S(1)} %get-tuple-element.29.index, f32[32,16384]{1,0:T(8,128)} %xfactor.3, f32[32,4096]{1,0:T(8,128)S(1)} %collective-permute-done.refs_0_, ...), custom_call_target="tpu_custom_call" | custom-call | flops 8999999488 | bytes 8388608 | tf_op jit(solution)/shard_map/transport_first/pallas_call | solution.py:181
  50.1 1.4 %collective-permute-start.7 = (f32[640,128]{1,0:T(8,128)S(1)}, f32[640,128]{1,0:T(8,128)S(1)}, u32[]{:S(2)}, u32[]{:S(2)}) collective-permute-start(f32[640,128]{1,0:T(8,128)S(1)} %get-tuple-element.11), channel_id=1, source_target_pairs={{0,4},{4,0},{1,5},{5,1},{2,6},{6,2},{3,7},{7,3},{8,12},{12,8},{9,1... | collective-permute-start | bytes 983048 | tf_op jit(solution)/shard_map/ppermute | solution.py:371
  52.8 2.5 %collective-permute-start.10 = (f32[160,128]{1,0:T(8,128)S(1)}, f32[160,128]{1,0:T(8,128)S(1)}, u32[]{:S(2)}, u32[]{:S(2)}) collective-permute-start(f32[160,128]{1,0:T(8,128)S(1)} %get-tuple-element.25), channel_id=1, source_target_pairs={{0,96},{32,0},{64,32},{96,64},{1,97},{33,1},{65,33},{97,65},{2,98}... | collective-permute-start | bytes 245768 | tf_op jit(solution)/shard_map/ppermute | solution.py:371
  56.9 3.4 %collective-permute-done.8 = f32[160,128]{1,0:T(8,128)S(1)} collective-permute-done((f32[160,128]{1,0:T(8,128)S(1)}, f32[160,128]{1,0:T(8,128)S(1)}, u32[]{:S(2)}, u32[]{:S(2)}) %collective-permute-start.8) | collective-permute-done | bytes 81952 | tf_op jit(solution)/shard_map/ppermute | solution.py:371
  60.2 2.3 %collective-permute-done.9 = f32[160,128]{1,0:T(8,128)S(1)} collective-permute-done((f32[160,128]{1,0:T(8,128)S(1)}, f32[160,128]{1,0:T(8,128)S(1)}, u32[]{:S(2)}, u32[]{:S(2)}) %collective-permute-start.9) | collective-permute-done | bytes 81952 | tf_op jit(solution)/shard_map/ppermute | solution.py:371
  62.6 2.8 %collective-permute-start.11 = (f32[160,128]{1,0:T(8,128)S(1)}, f32[160,128]{1,0:T(8,128)S(1)}, u32[]{:S(2)}, u32[]{:S(2)}) collective-permute-start(f32[160,128]{1,0:T(8,128)S(1)} %fusion), channel_id=1, source_target_pairs={{0,24},{8,0},{16,8},{24,16},{1,25},{9,1},{17,9},{25,17},{2,26},{10... | collective-permute-start | bytes 245768 | tf_op jit(solution)/shard_map/ppermute | solution.py:371
  65.4 1.6 %collective-permute-start.13 = (f32[160,128]{1,0:T(8,128)S(1)}, f32[160,128]{1,0:T(8,128)S(1)}, u32[]{:S(2)}, u32[]{:S(2)}) collective-permute-start(f32[160,128]{1,0:T(8,128)S(1)} %fusion), channel_id=1, source_target_pairs={{0,16},{8,24},{16,0},{24,8},{1,17},{9,25},{17,1},{25,9},{2,18},{10... | collective-permute-start | bytes 245768 | tf_op jit(solution)/shard_map/ppermute | solution.py:371
  67.0 3.7 %collective-permute-done.12 = f32[160,128]{1,0:T(8,128)S(1)} collective-permute-done((f32[160,128]{1,0:T(8,128)S(1)}, f32[160,128]{1,0:T(8,128)S(1)}, u32[]{:S(2)}, u32[]{:S(2)}) %collective-permute-start.12) | collective-permute-done | bytes 81952 | tf_op jit(solution)/shard_map/ppermute | solution.py:371
  70.8 2.4 %collective-permute-start.14 = (f32[160,128]{1,0:T(8,128)S(1)}, f32[160,128]{1,0:T(8,128)S(1)}, u32[]{:S(2)}, u32[]{:S(2)}) collective-permute-start(f32[160,128]{1,0:T(8,128)S(1)} %add_add_fusion.1), channel_id=1, source_target_pairs={{0,3},{1,0},{2,1},{3,2},{4,7},{5,4},{6,5},{7,6},{8,11},{9,8},{10,9... | collective-permute-start | bytes 245768 | tf_op jit(solution)/shard_map/ppermute | solution.py:371
  74.7 3.9 %collective-permute-done.15 = f32[160,128]{1,0:T(8,128)S(1)} collective-permute-done((f32[160,128]{1,0:T(8,128)S(1)}, f32[160,128]{1,0:T(8,128)S(1)}, u32[]{:S(2)}, u32[]{:S(2)}) %collective-permute-start.15) | collective-permute-done | bytes 81952 | tf_op jit(solution)/shard_map/ppermute | solution.py:371
  80.2 1.8 %collective-permute-done.17 = f32[160,128]{1,0:T(8,128)S(1)} collective-permute-done((f32[160,128]{1,0:T(8,128)S(1)}, f32[160,128]{1,0:T(8,128)S(1)}, u32[]{:S(2)}, u32[]{:S(2)}) %collective-permute-start.17) | collective-permute-done | bytes 81952 | tf_op jit(solution)/shard_map/ppermute | solution.py:371
  82.0 1.6 %collective-permute-done.18 = f32[160,128]{1,0:T(8,128)S(1)} collective-permute-done((f32[160,128]{1,0:T(8,128)S(1)}, f32[160,128]{1,0:T(8,128)S(1)}, u32[]{:S(2)}, u32[]{:S(2)}) %collective-permute-start.18) | collective-permute-done | bytes 81952 | tf_op jit(solution)/shard_map/ppermute | solution.py:371
  84.6 5.4 %collective-permute-start.20 = (f32[640,128]{1,0:T(8,128)S(1)}, f32[640,128]{1,0:T(8,128)S(1)}, u32[]{:S(2)}, u32[]{:S(2)}) collective-permute-start(f32[640,128]{1,0:T(8,128)S(1)} %bitcast.25), channel_id=1, source_target_pairs={{0,4},{4,0},{1,5},{5,1},{2,6},{6,2},{3,7},{7,3},{8,12},{12,8},{9,1... | collective-permute-start | bytes 983048 | tf_op jit(solution)/shard_map/ppermute | solution.py:371
  91.2 21.6 %factor.1 = (f32[512,512]{1,0:T(8,128)}, f32[128,4096]{1,0:T(8,128)}) custom-call(s32[1]{0:T(128)} %bitcast.place, f32[640,128]{1,0:T(8,128)S(1)} %bitcast.26, f32[640,128]{1,0:T(8,128)S(1)} %collective-permute-done.20.other, f32[512,128]{1,0:T(8,128)S(1)} %copy-done.1, bf16[2,512,2048]{2,1,0:T(8,128)(2,1)} %get-tuple-element.12.cand_first, ...), custom_call_target="tpu_custom_call" | custom-call | tf_op jit(solution)/shard_map/factor/pallas_call | solution.py:345
  (47 shorter events, 11.4 us)
Async XLA Ops:
  2.2 28.8 %copy-start.2 = (f32[3,64,64]{2,1,0:T(8,128)S(1)}, f32[3,64,64]{2,1,0:T(8,128)}, u32[]{:S(2)}) copy-start(f32[3,64,64]{2,1,0:T(8,128)} %refs_8_.1) | copy-start | bytes 147460
  2.2 28.8 %copy-start.3 = (f32[3,64,64]{2,1,0:T(8,128)S(1)}, f32[3,64,64]{2,1,0:T(8,128)}, u32[]{:S(2)}) copy-start(f32[3,64,64]{2,1,0:T(8,128)} %refs_9_.1) | copy-start | bytes 147460
  2.2 19.1 %collective-permute-start = (f32[32,4096]{1,0:T(8,128)S(1)}, f32[32,4096]{1,0:T(8,128)S(1)}, u32[]{:S(2)}, u32[]{:S(2)}) collective-permute-start(f32[32,4096]{1,0:T(8,128)S(1)} %get-tuple-element.24), channel_id=1, source_target_pairs={{0,2},{1,3},{2,0},{3,1},{4,6},{5,7},{6,4},{7,5},{8,10},{9,11},{10,... | collective-permute-start | bytes 1572872 | tf_op jit(solution)/shard_map/ppermute | solution.py:371
  6.7 24.3 %collective-permute-start.1 = (f32[32,4096]{1,0:T(8,128)S(1)}, f32[32,4096]{1,0:T(8,128)S(1)}, u32[]{:S(2)}, u32[]{:S(2)}) collective-permute-start(f32[32,4096]{1,0:T(8,128)S(1)} %get-tuple-element.23), channel_id=1, source_target_pairs={{0,1},{1,2},{2,3},{3,0},{4,5},{5,6},{6,7},{7,4},{8,9},{9,10},{10,1... | collective-permute-start | bytes 1572872 | tf_op jit(solution)/shard_map/ppermute | solution.py:371
  7.4 23.6 %collective-permute-start.2 = (f32[32,4096]{1,0:T(8,128)S(1)}, f32[32,4096]{1,0:T(8,128)S(1)}, u32[]{:S(2)}, u32[]{:S(2)}) collective-permute-start(f32[32,4096]{1,0:T(8,128)S(1)} %get-tuple-element.22), channel_id=1, source_target_pairs={{0,3},{1,0},{2,1},{3,2},{4,7},{5,4},{6,5},{7,6},{8,11},{9,8},{10,9... | collective-permute-start | bytes 1572872 | tf_op jit(solution)/shard_map/ppermute | solution.py:371
  11.0 8.2 %collective-permute-start.3 = (f32[32,2048]{1,0:T(8,128)}, f32[32,2048]{1,0:T(8,128)}, u32[]{:S(2)}, u32[]{:S(2)}) collective-permute-start(f32[32,2048]{1,0:T(8,128)} %slice.10), channel_id=1, source_target_pairs={{0,4},{4,8},{8,12},{12,16},{16,20},{20,24},{24,28},{28,32},{32,36}... | collective-permute-start | bytes 786440 | tf_op jit(solution)/shard_map/ppermute | solution.py:422
  20.9 19.6 %collective-permute-start.4 = (f32[32,2048]{1,0:T(8,128)S(1)}, f32[32,2048]{1,0:T(8,128)S(1)}, u32[]{:S(2)}, u32[]{:S(2)}) collective-permute-start(f32[32,2048]{1,0:T(8,128)S(1)} %get-tuple-element.20), channel_id=1, source_target_pairs={{0,2},{1,3},{2,0},{3,1},{4,6},{5,7},{6,4},{7,5},{8,10},{9,11},{10,... | collective-permute-start | bytes 786440 | tf_op jit(solution)/shard_map/ppermute | solution.py:371
  21.0 20.6 %collective-permute-start.5 = (f32[32,2048]{1,0:T(8,128)S(1)}, f32[32,2048]{1,0:T(8,128)S(1)}, u32[]{:S(2)}, u32[]{:S(2)}) collective-permute-start(f32[32,2048]{1,0:T(8,128)S(1)} %get-tuple-element.19), channel_id=1, source_target_pairs={{0,1},{1,2},{2,3},{3,0},{4,5},{5,6},{6,7},{7,4},{8,9},{9,10},{10,1... | collective-permute-start | bytes 786440 | tf_op jit(solution)/shard_map/ppermute | solution.py:371
  21.3 20.3 %collective-permute-start.6 = (f32[32,2048]{1,0:T(8,128)S(1)}, f32[32,2048]{1,0:T(8,128)S(1)}, u32[]{:S(2)}, u32[]{:S(2)}) collective-permute-start(f32[32,2048]{1,0:T(8,128)S(1)} %get-tuple-element.18), channel_id=1, source_target_pairs={{0,3},{1,0},{2,1},{3,2},{4,7},{5,4},{6,5},{7,6},{8,11},{9,8},{10,9... | collective-permute-start | bytes 786440 | tf_op jit(solution)/shard_map/ppermute | solution.py:371
  50.1 41.1 %copy-start.1 = (f32[512,128]{1,0:T(8,128)S(1)}, f32[512,128]{1,0:T(8,128)}, u32[]{:S(2)}) copy-start(f32[512,128]{1,0:T(8,128)} %coeffs.1) | copy-start | bytes 786436
  50.1 2.6 %collective-permute-start.7 = (f32[640,128]{1,0:T(8,128)S(1)}, f32[640,128]{1,0:T(8,128)S(1)}, u32[]{:S(2)}, u32[]{:S(2)}) collective-permute-start(f32[640,128]{1,0:T(8,128)S(1)} %get-tuple-element.11), channel_id=1, source_target_pairs={{0,4},{4,0},{1,5},{5,1},{2,6},{6,2},{3,7},{7,3},{8,12},{12,8},{9,1... | collective-permute-start | bytes 983048 | tf_op jit(solution)/shard_map/ppermute | solution.py:371
  52.8 4.0 %collective-permute-start.10 = (f32[160,128]{1,0:T(8,128)S(1)}, f32[160,128]{1,0:T(8,128)S(1)}, u32[]{:S(2)}, u32[]{:S(2)}) collective-permute-start(f32[160,128]{1,0:T(8,128)S(1)} %get-tuple-element.25), channel_id=1, source_target_pairs={{0,96},{32,0},{64,32},{96,64},{1,97},{33,1},{65,33},{97,65},{2,98}... | collective-permute-start | bytes 245768 | tf_op jit(solution)/shard_map/ppermute | solution.py:371
  55.4 4.9 %collective-permute-start.8 = (f32[160,128]{1,0:T(8,128)S(1)}, f32[160,128]{1,0:T(8,128)S(1)}, u32[]{:S(2)}, u32[]{:S(2)}) collective-permute-start(f32[160,128]{1,0:T(8,128)S(1)} %get-tuple-element.27), channel_id=1, source_target_pairs={{0,64},{32,96},{64,0},{96,32},{1,65},{33,97},{65,1},{97,33},{2,66}... | collective-permute-start | bytes 245768 | tf_op jit(solution)/shard_map/ppermute | solution.py:371
  56.0 6.6 %collective-permute-start.9 = (f32[160,128]{1,0:T(8,128)S(1)}, f32[160,128]{1,0:T(8,128)S(1)}, u32[]{:S(2)}, u32[]{:S(2)}) collective-permute-start(f32[160,128]{1,0:T(8,128)S(1)} %get-tuple-element.26), channel_id=1, source_target_pairs={{0,32},{32,64},{64,96},{96,0},{1,33},{33,65},{65,97},{97,1},{2,34}... | collective-permute-start | bytes 245768 | tf_op jit(solution)/shard_map/ppermute | solution.py:371
  62.6 4.4 %collective-permute-start.11 = (f32[160,128]{1,0:T(8,128)S(1)}, f32[160,128]{1,0:T(8,128)S(1)}, u32[]{:S(2)}, u32[]{:S(2)}) collective-permute-start(f32[160,128]{1,0:T(8,128)S(1)} %fusion), channel_id=1, source_target_pairs={{0,24},{8,0},{16,8},{24,16},{1,25},{9,1},{17,9},{25,17},{2,26},{10... | collective-permute-start | bytes 245768 | tf_op jit(solution)/shard_map/ppermute | solution.py:371
  65.4 5.3 %collective-permute-start.12 = (f32[160,128]{1,0:T(8,128)S(1)}, f32[160,128]{1,0:T(8,128)S(1)}, u32[]{:S(2)}, u32[]{:S(2)}) collective-permute-start(f32[160,128]{1,0:T(8,128)S(1)} %fusion), channel_id=1, source_target_pairs={{0,8},{8,16},{16,24},{24,0},{1,9},{9,17},{17,25},{25,1},{2,10},{10... | collective-permute-start | bytes 245768 | tf_op jit(solution)/shard_map/ppermute | solution.py:371
  65.4 5.4 %collective-permute-start.13 = (f32[160,128]{1,0:T(8,128)S(1)}, f32[160,128]{1,0:T(8,128)S(1)}, u32[]{:S(2)}, u32[]{:S(2)}) collective-permute-start(f32[160,128]{1,0:T(8,128)S(1)} %fusion), channel_id=1, source_target_pairs={{0,16},{8,24},{16,0},{24,8},{1,17},{9,25},{17,1},{25,9},{2,18},{10... | collective-permute-start | bytes 245768 | tf_op jit(solution)/shard_map/ppermute | solution.py:371
  70.8 3.9 %collective-permute-start.14 = (f32[160,128]{1,0:T(8,128)S(1)}, f32[160,128]{1,0:T(8,128)S(1)}, u32[]{:S(2)}, u32[]{:S(2)}) collective-permute-start(f32[160,128]{1,0:T(8,128)S(1)} %add_add_fusion.1), channel_id=1, source_target_pairs={{0,3},{1,0},{2,1},{3,2},{4,7},{5,4},{6,5},{7,6},{8,11},{9,8},{10,9... | collective-permute-start | bytes 245768 | tf_op jit(solution)/shard_map/ppermute | solution.py:371
  73.2 5.4 %collective-permute-start.15 = (f32[160,128]{1,0:T(8,128)S(1)}, f32[160,128]{1,0:T(8,128)S(1)}, u32[]{:S(2)}, u32[]{:S(2)}) collective-permute-start(f32[160,128]{1,0:T(8,128)S(1)} %add_add_fusion.1), channel_id=1, source_target_pairs={{0,1},{1,2},{2,3},{3,0},{4,5},{5,6},{6,7},{7,4},{8,9},{9,10},{10,1... | collective-permute-start | bytes 245768 | tf_op jit(solution)/shard_map/ppermute | solution.py:371
  73.2 5.4 %collective-permute-start.16 = (f32[160,128]{1,0:T(8,128)S(1)}, f32[160,128]{1,0:T(8,128)S(1)}, u32[]{:S(2)}, u32[]{:S(2)}) collective-permute-start(f32[160,128]{1,0:T(8,128)S(1)} %add_add_fusion.1), channel_id=1, source_target_pairs={{0,2},{1,3},{2,0},{3,1},{4,6},{5,7},{6,4},{7,5},{8,10},{9,11},{10,... | collective-permute-start | bytes 245768 | tf_op jit(solution)/shard_map/ppermute | solution.py:371
  78.7 3.4 %collective-permute-start.17 = (f32[160,128]{1,0:T(8,128)S(1)}, f32[160,128]{1,0:T(8,128)S(1)}, u32[]{:S(2)}, u32[]{:S(2)}) collective-permute-start(f32[160,128]{1,0:T(8,128)S(1)} %get-tuple-element.17), channel_id=1, source_target_pairs={{0,96},{32,0},{64,32},{96,64},{1,97},{33,1},{65,33},{97,65},{2,98}... | collective-permute-start | bytes 245768 | tf_op jit(solution)/shard_map/ppermute | solution.py:371
  78.8 4.9 %collective-permute-start.18 = (f32[160,128]{1,0:T(8,128)S(1)}, f32[160,128]{1,0:T(8,128)S(1)}, u32[]{:S(2)}, u32[]{:S(2)}) collective-permute-start(f32[160,128]{1,0:T(8,128)S(1)} %get-tuple-element.17), channel_id=1, source_target_pairs={{0,64},{32,96},{64,0},{96,32},{1,65},{33,97},{65,1},{97,33},{2,66}... | collective-permute-start | bytes 245768 | tf_op jit(solution)/shard_map/ppermute | solution.py:371
  79.0 5.5 %collective-permute-start.19 = (f32[160,128]{1,0:T(8,128)S(1)}, f32[160,128]{1,0:T(8,128)S(1)}, u32[]{:S(2)}, u32[]{:S(2)}) collective-permute-start(f32[160,128]{1,0:T(8,128)S(1)} %get-tuple-element.17), channel_id=1, source_target_pairs={{0,32},{32,64},{64,96},{96,0},{1,33},{33,65},{65,97},{97,1},{2,34}... | collective-permute-start | bytes 245768 | tf_op jit(solution)/shard_map/ppermute | solution.py:371
  84.6 6.7 %collective-permute-start.20 = (f32[640,128]{1,0:T(8,128)S(1)}, f32[640,128]{1,0:T(8,128)S(1)}, u32[]{:S(2)}, u32[]{:S(2)}) collective-permute-start(f32[640,128]{1,0:T(8,128)S(1)} %bitcast.25), channel_id=1, source_target_pairs={{0,4},{4,0},{1,5},{5,1},{2,6},{6,2},{3,7},{7,3},{8,12},{12,8},{9,1... | collective-permute-start | bytes 983048 | tf_op jit(solution)/shard_map/ppermute | solution.py:371
  (2 other events, 15.9 us)
